TPU v7x, 512 devices: a whole 4x8x8 slice. The times are simulated.
512 devices in a mesh: tm: 32 (over y, x), tile: 16 (over z, core).
Axes of the slice: x: 4, y: 8, z: 8, core: 2. Of those that a mesh axis runs over, the one named last changes fastest.
Arguments:
- latents: bfloat16 [128, 64, 16, 384], P('tm', 'tile'), may hold values from -24 to 24
- first_gain: float32 [384], replicated, may hold values from 0.25 to 1.75
- first_bias: float32 [384], replicated, may hold values from -0.5 to 0.5
- first_kernel: bfloat16 [384, 3, 3, 3, 192], P('tile'), may hold values from -0.0625 to 0.0625
- second_gain: float32 [192], replicated, may hold values from 0.25 to 1.75
- second_bias: float32 [192], replicated, may hold values from -0.5 to 0.5
- second_kernel: bfloat16 [192, 3, 3, 3, 192], replicated, may hold values from -0.078125 to 0.078125
- skip_weight: bfloat16 [384, 192], replicated, may hold values from -0.3125 to 0.3125
- resample_kernel: bfloat16 [3, 3, 192, 96], replicated, may hold values from -0.15625 to 0.15625
- clip_spans: int32 [4], replicated, may hold values from 1 to 16, 32 in all
Outputs:
- upsampled: bfloat16 [128, 128, 16, 192], P('tm', 'tile')
All inputs are finite; a program needn't handle non-finite values.
Results may differ from a plain program's by a relative error of at most 0.0059.
Values may be sent and summed in bfloat16 or wider, within the bound.
A program may use at most 64 MiB of HBM per device.

v0:
```python
import jax
import jax.numpy as jnp
from jax import lax
from jax.sharding import PartitionSpec as P

GROUPS = 32


norm_eps = 1e-06


def extended_2(cells, sides, width):
    for axis, dim in sides:
        count = lax.axis_size(axis)
        ends = count - 1
        head = lax.slice_in_dim(cells, 0, width, axis=dim)
        tail = lax.slice_in_dim(cells, cells.shape[dim] - width, cells.shape[dim], axis=dim)
        cells = jnp.concatenate(
            [
                lax.ppermute(tail, axis, [(i, (i + 1) % count) for i in range(ends)]),
                cells,
                lax.ppermute(head, axis, [((i + 1) % count, i) for i in range(ends)]),
            ],
            axis=dim,
        )
    return cells


def from_behind(value, axis, steps):
    count = lax.axis_size(axis)
    leading, last = (max(0, -steps), min(count, count - steps))
    return lax.ppermute(value, axis, [(source, source + steps) for source in range(leading, last)])


def group_totals(volume):
    frames, height, width_cells, channels = volume.shape
    grouped = volume.astype(jnp.float32).reshape(
        frames, height * width_cells, GROUPS, channels // GROUPS
    )
    return (jnp.sum(grouped, axis=(1, 3)), jnp.sum(grouped * grouped, axis=(1, 3)))


def normalize(volume, totals, squares, entries, norm_gain, norm_bias):
    frames, height, width_cells, channels = volume.shape
    mean_value = totals / entries
    inv_scale = lax.rsqrt(squares / entries - mean_value * mean_value + norm_eps)
    grouped = volume.astype(jnp.float32).reshape(
        frames, height, width_cells, GROUPS, channels // GROUPS
    )
    normed = (grouped - mean_value[:, None, None, :, None]) * inv_scale[:, None, None, :, None]
    normed = normed.reshape(volume.shape) * norm_gain + norm_bias
    return jax.nn.silu(normed).astype(jnp.bfloat16)


def conv_terms(extended, kernel_all):
    out_frames = extended.shape[0] - 2
    out_rows = extended.shape[1] - 2
    out_cols = extended.shape[2] - 2
    width_in = extended.shape[3]
    running = jnp.zeros((out_frames * out_rows * out_cols, kernel_all.shape[-1]), jnp.float32)
    for tap_time in range(3):
        for tap_row in range(3):
            for tap_col in range(3):
                window = extended[
                    tap_time : tap_time + out_frames,
                    tap_row : tap_row + out_rows,
                    tap_col : tap_col + out_cols,
                ]
                running = running + jnp.dot(
                    window.reshape(-1, width_in),
                    kernel_all[:, tap_time, tap_row, tap_col],
                    preferred_element_type=jnp.float32,
                )
    return running


def conv_stacked(extended, kernel_part):
    out_frames = extended.shape[0] - 2
    out_rows = extended.shape[1] - 2
    out_cols = extended.shape[2] - 2
    width_in = extended.shape[3]
    windows = []
    for tap_time in range(3):
        for tap_row in range(3):
            for tap_col in range(3):
                windows.append(
                    extended[
                        tap_time : tap_time + out_frames,
                        tap_row : tap_row + out_rows,
                        tap_col : tap_col + out_cols,
                    ]
                )
    stacked = jnp.concatenate(windows, axis=-1).reshape(-1, 27 * width_in)
    flat_kernel = jnp.transpose(kernel_part, (1, 2, 3, 0, 4)).reshape(
        27 * width_in, kernel_part.shape[-1]
    )
    return jnp.dot(stacked, flat_kernel, preferred_element_type=jnp.float32)


def pad_columns(volume):
    return jnp.pad(volume, ((0, 0), (0, 0), (1, 1), (0, 0)))


def shards(
    latents,
    first_gain,
    first_bias,
    first_kernel,
    second_gain,
    second_bias,
    second_kernel,
    skip_weight,
    resample_kernel,
    clip_spans,
):
    frames, tile_rows, tile_cols, chans_in = latents.shape
    chans_mid = second_kernel.shape[-1]
    chans_out = resample_kernel.shape[-1]
    height = tile_rows * lax.axis_size("tile")
    tile_at = lax.axis_index("tile")
    span_at = lax.axis_index("tm")
    starts = jnp.cumsum(clip_spans) - clip_spans
    starts_here = jnp.any(starts == span_at)
    totals, squares = group_totals(latents)
    totals, squares = lax.psum((totals, squares), "tile")
    first_act = normalize(
        latents, totals, squares, height * tile_cols * (chans_in // GROUPS), first_gain, first_bias
    )
    first_rows = extended_2(first_act, (("tile", 1),), 1)
    handed = from_behind(first_rows[frames - 2 :], "tm", 1)
    handed = jnp.where(starts_here, jnp.zeros_like(handed), handed)
    first_ext = pad_columns(jnp.concatenate([handed, first_rows], axis=0))
    frames_first = first_ext.shape[0] - 2
    rows_first = first_ext.shape[1] - 2
    hidden_first = conv_stacked(first_ext, lax.all_gather(first_kernel, "tile", axis=0, tiled=True))
    hidden_first = hidden_first.reshape(frames_first, rows_first, tile_cols, chans_mid)
    offset = (rows_first - tile_rows) // 2
    totals, squares = group_totals(hidden_first)
    totals, squares = lax.psum((totals, squares), "tile")
    second_act = normalize(
        hidden_first,
        totals,
        squares,
        height * tile_cols * (chans_mid // GROUPS),
        second_gain,
        second_bias,
    )
    global_row = tile_at * tile_rows - offset + jnp.arange(rows_first)
    inside = (global_row >= 0) & (global_row < height)
    second_act = jnp.where(inside[None, :, None, None], second_act, jnp.zeros_like(second_act))
    second_rows = extended_2(second_act, (("tile", 1),), 1)
    handed_second = from_behind(second_rows[frames - 2 :], "tm", 1)
    handed_second = jnp.where(starts_here, jnp.zeros_like(handed_second), handed_second)
    second_ext = pad_columns(jnp.concatenate([handed_second, second_rows], axis=0))
    hidden_second = conv_terms(second_ext, second_kernel)
    shortcut = jnp.dot(
        latents.reshape(-1, chans_in), skip_weight, preferred_element_type=jnp.float32
    )
    block_out = (
        (hidden_second + shortcut)
        .astype(jnp.bfloat16)
        .reshape(frames, tile_rows, tile_cols, chans_mid)
    )
    block_rows = extended_2(block_out, (("tile", 1),), 1)
    padded_block = pad_columns(block_rows)
    enlarged = jnp.repeat(jnp.repeat(padded_block, 2, axis=1), 2, axis=2)
    enlarged = enlarged[:, 1 : 2 * tile_rows + 3, 1 : 2 * tile_cols + 3]
    running = jnp.zeros((frames * 4 * tile_rows * tile_cols, chans_out), jnp.float32)
    for tap_row in range(3):
        for tap_col in range(3):
            window = enlarged[
                :, tap_row : tap_row + 2 * tile_rows, tap_col : tap_col + 2 * tile_cols
            ]
            running = running + jnp.dot(
                window.reshape(-1, chans_mid),
                resample_kernel[tap_row, tap_col],
                preferred_element_type=jnp.float32,
            )
    return running.reshape(frames, 2 * tile_rows, tile_cols, 2 * chans_out).astype(jnp.bfloat16)


def solution(mesh):
    in_specs = (
        P("tm", "tile", None, None),
        P(),
        P(),
        P("tile", None, None, None, None),
        P(),
        P(),
        P(),
        P(),
        P(),
        P(),
    )
    out_specs = P("tm", "tile", None, None)
    return jax.shard_map(shards, mesh=mesh, in_specs=in_specs, out_specs=out_specs, check_vma=False)
```

profile of v0, /device:TPU:225, one launch (start us, length us, event | category | flops | bytes accessed | tf_op | source)
XLA Modules:
  0.0 169.0 jit_solution(16302599858866524232)
XLA Ops:
  7.3 1.0 convert_reduce_fusion
  8.7 24.4 %all-reduce.4 = (f32[4,32]{1,0:T(4,128)S(1)}, f32[4,32]{1,0:T(4,128)S(1)}) all-reduce(f32[4,32]{1,0:T(4,128)S(1)} %reduce_sum.55, f32[4,32]{1,0:T(4,128)S(1)} %reduce_sum.52), channel_id=1, replica_groups=mesh['tm'=32,'tile'=16] {'tile'}, use_global_device_ids=true, to_apply=%region_7.8 | all-reduce | flops 256 | bytes 2048 | tf_op jit(solution)/shard_map/psum | solution.py:125
  33.5 1.1 fusion.12
  34.6 5.4 %collective-permute-start = (bf16[4,1,16,384]{3,2,1,0:T(8,128)(2,1)S(1)}, bf16[4,1,16,384]{3,2,1,0:T(8,128)(2,1)S(1)}, u32[]{:S(2)}, u32[]{:S(2)}) collective-permute-start(bf16[4,1,16,384]{3,2,1,0:T(8,128)(2,1)S(1)} %get-tuple-element.46), channel_id=1, source_target_pairs={{0,1},{1,2},{2,3},{3,4},{4,5},{5,6},{6,7},{7,8},{8,9},{9,10},{10,1... | collective-permute-start | bytes 147464 | tf_op jit(solution)/shard_map/ppermute | solution.py:20
  40.0 1.9 %collective-permute-start.1 = (bf16[4,1,16,384]{3,2,1,0:T(8,128)(2,1)S(1)}, bf16[4,1,16,384]{3,2,1,0:T(8,128)(2,1)S(1)}, u32[]{:S(2)}, u32[]{:S(2)}) collective-permute-start(bf16[4,1,16,384]{3,2,1,0:T(8,128)(2,1)S(1)} %get-tuple-element.47), channel_id=1, source_target_pairs={{1,0},{2,1},{3,2},{4,3},{5,4},{6,5},{7,6},{8,7},{9,8},{10,9},{11,1... | collective-permute-start | bytes 147464 | tf_op jit(solution)/shard_map/ppermute | solution.py:22
  42.0 5.8 %collective-permute-done.1 = bf16[4,1,16,384]{3,2,1,0:T(8,128)(2,1)S(1)} collective-permute-done((bf16[4,1,16,384]{3,2,1,0:T(8,128)(2,1)S(1)}, bf16[4,1,16,384]{3,2,1,0:T(8,128)(2,1)S(1)}, u32[]{:S(2)}, u32[]{:S(2)}) %collective-permute-start.1) | collective-permute-done | bytes 49184 | tf_op jit(solution)/shard_map/ppermute | solution.py:22
  47.8 3.2 %collective-permute-start.2 = (bf16[2,6,16,384]{3,2,1,0:T(8,128)(2,1)S(1)}, bf16[2,6,16,384]{3,2,1,0:T(8,128)(2,1)S(1)}, u32[]{:S(2)}, u32[]{:S(2)}) collective-permute-start(bf16[2,6,16,384]{3,2,1,0:T(8,128)(2,1)S(1)} %pad_maximum_fusion.3), channel_id=1, source_target_pairs={{0,16},{16,32},{32,48},{48,64},{64,80},{80,96},{96,112},{112,128},... | collective-permute-start | bytes 442376 | tf_op jit(solution)/shard_map/ppermute | solution.py:32
  51.0 0.8 reduce-window.9
  51.8 1.3 compare_reduce_fusion
  53.2 3.9 %collective-permute-done.2 = bf16[2,6,16,384]{3,2,1,0:T(8,128)(2,1)S(1)} collective-permute-done((bf16[2,6,16,384]{3,2,1,0:T(8,128)(2,1)S(1)}, bf16[2,6,16,384]{3,2,1,0:T(8,128)(2,1)S(1)}, u32[]{:S(2)}, u32[]{:S(2)}) %collective-permute-start.2) | collective-permute-done | bytes 147488 | tf_op jit(solution)/shard_map/ppermute | solution.py:32
  57.8 0.8 fusion.14
  58.6 0.8 slice_dynamic-update-slice_fusion.5
  60.1 0.8 fusion.16
  61.5 0.8 fusion.17
  62.3 0.7 fusion.18
  63.8 0.8 fusion.19
  64.5 0.8 fusion.20
  66.0 0.8 fusion.21
  66.8 0.8 fusion.22
  68.2 0.7 fusion.23
  69.0 0.8 fusion.24
  70.5 0.7 fusion.25
  71.2 0.7 fusion.26
  72.7 0.8 fusion.27
  73.4 0.8 fusion.28
  74.2 0.8 constant_dynamic-update-slice_fusion
  75.0 0.8 fusion.29
  75.8 0.8 fusion.30
  76.6 0.7 fusion.32
  77.3 0.7 fusion.31
  78.0 6.4 %fusion.123 = f32[256,192]{0,1:T(8,128)S(1)} fusion(bf16[256,10368]{1,0:T(8,128)(2,1)} %bitcast.2, bf16[10368,192]{1,0:T(8,128)(2,1)} %bitcast.201), kind=kOutput, calls=%fused_computation.226 | convolution fusion | flops 1019215872 | bytes 9486336 | tf_op jit(solution)/shard_map/dot_general | solution.py:97
  84.5 0.9 reshape_reshape.7
  85.4 0.8 copy.54
  86.3 1.2 fusion.117
  87.7 23.0 %all-reduce.3 = (f32[4,32]{1,0:T(4,128)S(1)}, f32[4,32]{1,0:T(4,128)S(1)}) all-reduce(f32[4,32]{1,0:T(4,128)S(1)} %copy.56, f32[4,32]{1,0:T(4,128)S(1)} %copy.55), channel_id=1, replica_groups=mesh['tm'=32,'tile'=16] {'tile'}, use_global_device_ids=true, to_apply=%region_11.12 | all-reduce | flops 256 | bytes 2048 | tf_op jit(solution)/shard_map/psum | solution.py:139
  111.1 1.1 broadcast_select_fusion.1
  112.2 5.4 %collective-permute-start.3 = (bf16[4,1,16,192]{3,2,1,0:T(8,128)(2,1)S(1)}, bf16[4,1,16,192]{3,2,1,0:T(8,128)(2,1)S(1)}, u32[]{:S(2)}, u32[]{:S(2)}) collective-permute-start(bf16[4,1,16,192]{3,2,1,0:T(8,128)(2,1)S(1)} %get-tuple-element.52), channel_id=1, source_target_pairs={{0,1},{1,2},{2,3},{3,4},{4,5},{5,6},{6,7},{7,8},{8,9},{9,10},{10,1... | collective-permute-start | bytes 73736 | tf_op jit(solution)/shard_map/ppermute | solution.py:20
  117.6 1.9 %collective-permute-start.4 = (bf16[4,1,16,192]{3,2,1,0:T(8,128)(2,1)S(1)}, bf16[4,1,16,192]{3,2,1,0:T(8,128)(2,1)S(1)}, u32[]{:S(2)}, u32[]{:S(2)}) collective-permute-start(bf16[4,1,16,192]{3,2,1,0:T(8,128)(2,1)S(1)} %get-tuple-element.53), channel_id=1, source_target_pairs={{1,0},{2,1},{3,2},{4,3},{5,4},{6,5},{7,6},{8,7},{9,8},{10,9},{11,1... | collective-permute-start | bytes 73736 | tf_op jit(solution)/shard_map/ppermute | solution.py:22
  119.7 0.7 sub.48
  120.4 1.7 %copy.57 = f32[256,192]{0,1:T(8,128)} copy(f32[256,192]{1,0:T(8,128)} %bitcast.214) | data formatting | bytes 393216 | tf_op jit(solution)/shard_map/sub | solution.py:50
  122.9 1.7 %copy.58 = f32[256,192]{0,1:T(8,128)} copy(f32[256,192]{1,0:T(8,128)} %bitcast.215) | data formatting | bytes 393216 | tf_op jit(solution)/shard_map/mul | solution.py:50
  124.6 1.9 %collective-permute-start.5 = (bf16[2,6,16,192]{3,2,1,0:T(8,128)(2,1)S(1)}, bf16[2,6,16,192]{3,2,1,0:T(8,128)(2,1)S(1)}, u32[]{:S(2)}, u32[]{:S(2)}) collective-permute-start(bf16[2,6,16,192]{3,2,1,0:T(8,128)(2,1)S(1)} %pad_maximum_fusion.7), channel_id=1, source_target_pairs={{0,16},{16,32},{32,48},{48,64},{64,80},{80,96},{96,112},{112,128},... | collective-permute-start | bytes 221192 | tf_op jit(solution)/shard_map/ppermute | solution.py:32
  126.6 6.7 %collective-permute-done.5 = bf16[2,6,16,192]{3,2,1,0:T(8,128)(2,1)S(1)} collective-permute-done((bf16[2,6,16,192]{3,2,1,0:T(8,128)(2,1)S(1)}, bf16[2,6,16,192]{3,2,1,0:T(8,128)(2,1)S(1)}, u32[]{:S(2)}, u32[]{:S(2)}) %collective-permute-start.5) | collective-permute-done | bytes 73760 | tf_op jit(solution)/shard_map/ppermute | solution.py:32
  141.7 6.0 %collective-permute-start.6 = (bf16[4,1,16,192]{3,2,1,0:T(8,128)(2,1)S(1)}, bf16[4,1,16,192]{3,2,1,0:T(8,128)(2,1)S(1)}, u32[]{:S(2)}, u32[]{:S(2)}) collective-permute-start(bf16[4,1,16,192]{3,2,1,0:T(8,128)(2,1)S(1)} %get-tuple-element.48), channel_id=1, source_target_pairs={{0,1},{1,2},{2,3},{3,4},{4,5},{5,6},{6,7},{7,8},{8,9},{9,10},{10,1... | collective-permute-start | bytes 73736 | tf_op jit(solution)/shard_map/ppermute | solution.py:20
  147.7 2.1 %collective-permute-start.7 = (bf16[4,1,16,192]{3,2,1,0:T(8,128)(2,1)S(1)}, bf16[4,1,16,192]{3,2,1,0:T(8,128)(2,1)S(1)}, u32[]{:S(2)}, u32[]{:S(2)}) collective-permute-start(bf16[4,1,16,192]{3,2,1,0:T(8,128)(2,1)S(1)} %get-tuple-element.49), channel_id=1, source_target_pairs={{1,0},{2,1},{3,2},{4,3},{5,4},{6,5},{7,6},{8,7},{9,8},{10,9},{11,1... | collective-permute-start | bytes 73736 | tf_op jit(solution)/shard_map/ppermute | solution.py:22
  149.8 4.3 %collective-permute-done.7 = bf16[4,1,16,192]{3,2,1,0:T(8,128)(2,1)S(1)} collective-permute-done((bf16[4,1,16,192]{3,2,1,0:T(8,128)(2,1)S(1)}, bf16[4,1,16,192]{3,2,1,0:T(8,128)(2,1)S(1)}, u32[]{:S(2)}, u32[]{:S(2)}) %collective-permute-start.7) | collective-permute-done | bytes 24608 | tf_op jit(solution)/shard_map/ppermute | solution.py:22
  154.8 2.6 %fusion.118 = (bf16[4,8,32,192]{3,0,2,1:T(4,128)(2,1)S(1)}, bf16[4,8,32,192]{3,0,2,1:T(4,128)(2,1)S(1)}, bf16[4,8,32,192]{3,0,2,1:T(4,128)(2,1)S(1)}, bf16[4,8,3...) fusion(bf16[4,12,36,192]{3,0,2,1:T(4,128)(2,1)S(1)} %bitcast.200), kind=kLoop, calls=%fused_computation.221 | loop fusion | bytes 7077888 | tf_op jit(solution)/shard_map/slice | solution.py:171
  161.3 0.9 convert_element_type.34
  (119 shorter events, 21.3 us)
Async XLA Ops:
  6.5 134.8 %copy-start = (bf16[384,192]{0,1:T(8,128)(2,1)S(1)}, bf16[384,192]{0,1:T(8,128)(2,1)}, u32[]{:S(2)}) copy-start(bf16[384,192]{0,1:T(8,128)(2,1)} %param.17) | copy-start | bytes 442372
  6.5 71.5 %all-gather.2.cloned.1.call-start = ((), (), s32[]{:S(2)}) async-start(), calls=%async_computation | async-start | bytes 5640192 | tf_op jit(solution)/shard_map/all_gather | solution.py:135
  34.6 7.4 %collective-permute-start = (bf16[4,1,16,384]{3,2,1,0:T(8,128)(2,1)S(1)}, bf16[4,1,16,384]{3,2,1,0:T(8,128)(2,1)S(1)}, u32[]{:S(2)}, u32[]{:S(2)}) collective-permute-start(bf16[4,1,16,384]{3,2,1,0:T(8,128)(2,1)S(1)} %get-tuple-element.46), channel_id=1, source_target_pairs={{0,1},{1,2},{2,3},{3,4},{4,5},{5,6},{6,7},{7,8},{8,9},{9,10},{10,1... | collective-permute-start | bytes 147464 | tf_op jit(solution)/shard_map/ppermute | solution.py:20
  40.0 7.8 %collective-permute-start.1 = (bf16[4,1,16,384]{3,2,1,0:T(8,128)(2,1)S(1)}, bf16[4,1,16,384]{3,2,1,0:T(8,128)(2,1)S(1)}, u32[]{:S(2)}, u32[]{:S(2)}) collective-permute-start(bf16[4,1,16,384]{3,2,1,0:T(8,128)(2,1)S(1)} %get-tuple-element.47), channel_id=1, source_target_pairs={{1,0},{2,1},{3,2},{4,3},{5,4},{6,5},{7,6},{8,7},{9,8},{10,9},{11,1... | collective-permute-start | bytes 147464 | tf_op jit(solution)/shard_map/ppermute | solution.py:22
  47.8 9.2 %collective-permute-start.2 = (bf16[2,6,16,384]{3,2,1,0:T(8,128)(2,1)S(1)}, bf16[2,6,16,384]{3,2,1,0:T(8,128)(2,1)S(1)}, u32[]{:S(2)}, u32[]{:S(2)}) collective-permute-start(bf16[2,6,16,384]{3,2,1,0:T(8,128)(2,1)S(1)} %pad_maximum_fusion.3), channel_id=1, source_target_pairs={{0,16},{16,32},{32,48},{48,64},{64,80},{80,96},{96,112},{112,128},... | collective-permute-start | bytes 442376 | tf_op jit(solution)/shard_map/ppermute | solution.py:32
  60.1 14.1 %copy-start.1 = (bf16[4,4,16,384]{3,2,1,0:T(8,128)(2,1)S(1)}, bf16[4,4,16,384]{3,2,1,0:T(8,128)(2,1)}, u32[]{:S(2)}) copy-start(bf16[4,4,16,384]{3,2,1,0:T(8,128)(2,1)} %param.10) | copy-start | bytes 589828
  60.1 14.1 %copy-start.6 = (f32[384]{0:T(512)S(1)}, f32[384]{0:T(512)}, u32[]{:S(2)}) copy-start(f32[384]{0:T(512)} %param.12) | copy-start | bytes 4612
  60.1 14.1 %copy-start.7 = (f32[384]{0:T(512)S(1)}, f32[384]{0:T(512)}, u32[]{:S(2)}) copy-start(f32[384]{0:T(512)} %param.11) | copy-start | bytes 4612
  78.0 33.0 %copy-start.8 = (f32[192]{0:T(256)S(1)}, f32[192]{0:T(256)}, u32[]{:S(2)}) copy-start(f32[192]{0:T(256)} %param.15) | copy-start | bytes 2308
  78.0 33.0 %copy-start.9 = (f32[192]{0:T(256)S(1)}, f32[192]{0:T(256)}, u32[]{:S(2)}) copy-start(f32[192]{0:T(256)} %param.14) | copy-start | bytes 2308
  84.5 50.1 %copy-start.2 = (bf16[192,3,3,3,192]{4,0,3,2,1:T(8,128)(2,1)S(1)}, bf16[192,3,3,3,192]{4,0,3,2,1:T(8,128)(2,1)}, u32[]{:S(2)}) copy-start(bf16[192,3,3,3,192]{4,0,3,2,1:T(8,128)(2,1)} %param.16) | copy-start | bytes 5971972
  112.2 12.4 %collective-permute-start.3 = (bf16[4,1,16,192]{3,2,1,0:T(8,128)(2,1)S(1)}, bf16[4,1,16,192]{3,2,1,0:T(8,128)(2,1)S(1)}, u32[]{:S(2)}, u32[]{:S(2)}) collective-permute-start(bf16[4,1,16,192]{3,2,1,0:T(8,128)(2,1)S(1)} %get-tuple-element.52), channel_id=1, source_target_pairs={{0,1},{1,2},{2,3},{3,4},{4,5},{5,6},{6,7},{7,8},{8,9},{9,10},{10,1... | collective-permute-start | bytes 73736 | tf_op jit(solution)/shard_map/ppermute | solution.py:20
  117.6 7.0 %collective-permute-start.4 = (bf16[4,1,16,192]{3,2,1,0:T(8,128)(2,1)S(1)}, bf16[4,1,16,192]{3,2,1,0:T(8,128)(2,1)S(1)}, u32[]{:S(2)}, u32[]{:S(2)}) collective-permute-start(bf16[4,1,16,192]{3,2,1,0:T(8,128)(2,1)S(1)} %get-tuple-element.53), channel_id=1, source_target_pairs={{1,0},{2,1},{3,2},{4,3},{5,4},{6,5},{7,6},{8,7},{9,8},{10,9},{11,1... | collective-permute-start | bytes 73736 | tf_op jit(solution)/shard_map/ppermute | solution.py:22
  124.6 8.7 %collective-permute-start.5 = (bf16[2,6,16,192]{3,2,1,0:T(8,128)(2,1)S(1)}, bf16[2,6,16,192]{3,2,1,0:T(8,128)(2,1)S(1)}, u32[]{:S(2)}, u32[]{:S(2)}) collective-permute-start(bf16[2,6,16,192]{3,2,1,0:T(8,128)(2,1)S(1)} %pad_maximum_fusion.7), channel_id=1, source_target_pairs={{0,16},{16,32},{32,48},{48,64},{64,80},{80,96},{96,112},{112,128},... | collective-permute-start | bytes 221192 | tf_op jit(solution)/shard_map/ppermute | solution.py:32
  136.0 4.2 %copy-start.4 = (f32[256,192]{0,1:T(8,128)S(1)}, f32[256,192]{0,1:T(8,128)}, u32[]{:S(2)}) copy-start(f32[256,192]{0,1:T(8,128)} %copy.57) | copy-start | bytes 589828
  136.1 4.2 %copy-start.5 = (f32[256,192]{0,1:T(8,128)S(1)}, f32[256,192]{0,1:T(8,128)}, u32[]{:S(2)}) copy-start(f32[256,192]{0,1:T(8,128)} %copy.58) | copy-start | bytes 589828
  141.7 8.1 %collective-permute-start.6 = (bf16[4,1,16,192]{3,2,1,0:T(8,128)(2,1)S(1)}, bf16[4,1,16,192]{3,2,1,0:T(8,128)(2,1)S(1)}, u32[]{:S(2)}, u32[]{:S(2)}) collective-permute-start(bf16[4,1,16,192]{3,2,1,0:T(8,128)(2,1)S(1)} %get-tuple-element.48), channel_id=1, source_target_pairs={{0,1},{1,2},{2,3},{3,4},{4,5},{5,6},{6,7},{7,8},{8,9},{9,10},{10,1... | collective-permute-start | bytes 73736 | tf_op jit(solution)/shard_map/ppermute | solution.py:20
  147.7 6.4 %collective-permute-start.7 = (bf16[4,1,16,192]{3,2,1,0:T(8,128)(2,1)S(1)}, bf16[4,1,16,192]{3,2,1,0:T(8,128)(2,1)S(1)}, u32[]{:S(2)}, u32[]{:S(2)}) collective-permute-start(bf16[4,1,16,192]{3,2,1,0:T(8,128)(2,1)S(1)} %get-tuple-element.49), channel_id=1, source_target_pairs={{1,0},{2,1},{3,2},{4,3},{5,4},{6,5},{7,6},{8,7},{9,8},{10,9},{11,1... | collective-permute-start | bytes 73736 | tf_op jit(solution)/shard_map/ppermute | solution.py:22
  157.4 1.0 copy-start.3
Sparse Core Ops, SparseCore 0:
  9.5 48.4 all-gather.1
where the time goes:
time: 170 us; the launch traced here: 169 us
  blocking collectives  47.4 us (28%)
  local copies, waits for them, and re-layouts  31.8 us (19%)
  starting transfers between devices  27.8 us (16%)
  waiting for transfers between devices  21.4 us (13%)
  matrix products  15.8 us (9%)
  between operations  14.1 us (8%)
  other arithmetic  10.6 us (6%)
    psum x2, blocking collectives, shards(): totals, squares = lax.psum((totals, squares), 'tile')  47.4 us
    unnamed x44, local copies, waits for them, and re-layouts  17.6 us
    ppermute x3, starting transfers between devices, extended_2(): lax.ppermute(tail, axis, [(i, (i + 1) % count) for i in range(ends)])  16.8 us
    ppermute x2, waiting for transfers between devices, from_behind(): lax.ppermute(value, axis, [(source, source + steps) for source in range(l...  10.6 us
    ppermute x3, waiting for transfers between devices, extended_2(): lax.ppermute(head, axis, [((i + 1) % count, i) for i in range(ends)])  10.2 us
    dot_general x27, matrix products, conv_terms(): jnp.dot(window.reshape(-1, width_in), kernel_all[:, tap_time, tap_row, ta...  6.48 us
    dot_general x1, matrix products, conv_stacked(): return jnp.dot(stacked, flat_kernel, preferred_element_type=jnp.float32)  6.43 us
    ppermute x3, starting transfers between devices, extended_2(): lax.ppermute(head, axis, [((i + 1) % count, i) for i in range(ends)])  5.94 us
  transfers between devices with their start and end apart: 9, of which 4 were waited for; matrix products, arithmetic and copies ran while one was open for 18% of the time, Pallas kernels for 0%

commit v1 on v0

v1 whole, which is shorter than its diff:
```python
import functools

import jax
import jax.numpy as jnp
from jax import lax
from jax.experimental import pallas as pl
from jax.experimental.pallas import tpu as pltpu
from jax.sharding import PartitionSpec as P

GROUPS = 32
EPS = 1e-6
F32 = jnp.float32
BF16 = jnp.bfloat16
HIGHEST = lax.Precision.HIGHEST

FR, ROWS, COLS = 4, 4, 16
CIN, CMID, COUT = 384, 192, 96
SPANS, TILES = 32, 16
NX, NY, NZ = 4, 8, 8
SHARD = CIN // TILES
UNIT = 2 * SHARD
XT, YT = 12, 8
ZT = 27 - XT - YT
HEIGHT = ROWS * TILES


def member(per, transposed):
    channels = per * GROUPS
    shape = (128, channels) if transposed else (channels, 128)
    lane = lax.broadcasted_iota(jnp.int32, shape, 0 if transposed else 1)
    chan = lax.broadcasted_iota(jnp.int32, shape, 1 if transposed else 0)
    first = jnp.bitwise_and(lane, GROUPS - 1) * per
    return jnp.where((chan >= first) & (chan < first + per), 1.0, 0.0).astype(F32)


def frame_lanes(rows):
    lane = lax.broadcasted_iota(jnp.int32, (rows, 128), 1)
    row = lax.broadcasted_iota(jnp.int32, (rows, 128), 0)
    low = jnp.bitwise_and(row, FR - 1) * GROUPS
    return (lane >= low) & (lane < low + GROUPS)


def partial_stats(sums, squares, per):
    both = jnp.concatenate([sums, squares], axis=0)
    wide = jnp.dot(both, member(per, False), precision=HIGHEST, preferred_element_type=F32)
    wide = jnp.where(frame_lanes(2 * FR), wide, 0.0)
    return jnp.concatenate(
        [jnp.sum(wide[:FR], axis=0, keepdims=True), jnp.sum(wide[FR:], axis=0, keepdims=True)], axis=0
    )


def affine(total, total_prev, gain, bias, per):
    entries = float(HEIGHT * COLS * per)

    def rows_of(message):
        mean = message[0:1] / entries
        inv = lax.rsqrt(message[1:2] / entries - mean * mean + EPS)
        return [jnp.broadcast_to(mean, (FR, 128)), jnp.broadcast_to(inv, (FR, 128))]

    stacked = jnp.concatenate(rows_of(total) + rows_of(total_prev), axis=0)
    stacked = jnp.where(frame_lanes(4 * FR), stacked, 0.0)
    wide = jnp.dot(stacked, member(per, True), precision=HIGHEST, preferred_element_type=F32)
    out = []
    for at in (0, 2 * FR):
        scale = wide[at + FR : at + 2 * FR] * gain
        out.append((scale, bias - wide[at : at + FR] * scale))
    return out


def silu(v):
    half = 0.5 * v
    return half + half * jnp.tanh(half)


def shifted(a):
    zero = jnp.zeros(a.shape[:1] + (1,) + a.shape[2:], a.dtype)
    left = jnp.concatenate([zero, a[:, : COLS - 1]], axis=1)
    right = jnp.concatenate([a[:, 1:], zero], axis=1)
    return left, a, right


def kernel(
    lat, g1, b1, fk, g2, b2, sk, skw, rk, clips, out,
    xraw, fk_in, fk_pair, w1, w2, wskip, rkv, x1, hown, hraw, x2, x3, wres, acc_ref, out_v,
    mine, st_in, st_prev, mine2, st_in2, st_prev2,
    load_sem, halo_s, halo_r, stat_s, stat_r, pair_s, pair_r,
    zs, zr, xs, xr, ys, yr, ps, pr,
):
    tm = lax.axis_index("tm")
    tile = lax.axis_index("tile")
    y, x = tm // NX, lax.rem(tm, NX)
    z, core = tile // 2, lax.rem(tile, 2)
    step = 1 - 2 * core
    tm_next, tm_prev = lax.rem(tm + 1, SPANS), lax.rem(tm + SPANS - 1, SPANS)
    up, down = lax.rem(tile + TILES - 1, TILES), lax.rem(tile + 1, TILES)
    partner = (tm, tile + step)

    def along_x(by):
        return (y * NX + lax.rem(x + by + 2 * NX, NX), tile)

    def along_y(by):
        return (lax.rem(y + by + 2 * NY, NY) * NX + x, tile)

    def along_z(by):
        return (tm, lax.rem(z + by + 2 * NZ, NZ) * 2 + core)

    def remote(src, dst, send, recv, to):
        return pltpu.make_async_remote_copy(
            src_ref=src, dst_ref=dst, send_sem=send, recv_sem=recv,
            device_id=to, device_id_type=pl.DeviceIdType.MESH,
        )

    loads = [
        pltpu.make_async_copy(lat, xraw.at[2:6, 1:5], load_sem.at[0]),
        pltpu.make_async_copy(fk, fk_in, load_sem.at[1]),
        pltpu.make_async_copy(sk, w2, load_sem.at[2]),
        pltpu.make_async_copy(skw, wskip, load_sem.at[3]),
        pltpu.make_async_copy(rk, rkv, load_sem.at[4]),
    ]
    for load in loads:
        load.start()

    barrier = pltpu.get_barrier_semaphore()

    def greet(to):
        pl.semaphore_signal(barrier, inc=1, device_id=to, device_id_type=pl.DeviceIdType.MESH)

    def greet_group(i, carry):
        greet((tm, lax.rem(tile + i, TILES)))
        return carry

    def greet_prev(i, carry):
        greet((tm_prev, lax.rem(tile + i, TILES)))
        return carry

    lax.fori_loop(1, TILES, greet_group, 0)
    lax.fori_loop(0, TILES, greet_prev, 0)
    x_steps = (1, -1)
    for by in x_steps:
        greet(along_x(by))
    for by in x_steps:
        greet(along_y(by))

    loads[0].wait()
    sums, squares = [], []
    for f in range(FR):
        v = xraw[2 + f, 1:5].astype(F32).reshape(ROWS * COLS, CIN)
        sums.append(jnp.sum(v, axis=0, keepdims=True))
        squares.append(jnp.sum(v * v, axis=0, keepdims=True))
    mine[...] = partial_stats(jnp.concatenate(sums), jnp.concatenate(squares), CIN // GROUPS)
    loads[1].wait()
    pl.semaphore_wait(barrier, TILES - 1 + TILES + 4)

    def exchange(src, at_in, at_prev, phase):
        def to_group(i, carry):
            remote(
                src, at_in.at[i - 1], stat_s.at[phase, 0], stat_r.at[phase, 0],
                (tm, lax.rem(tile + i, TILES)),
            ).start()
            return carry

        def to_next(i, carry):
            remote(
                src, at_prev.at[i], stat_s.at[phase, 1], stat_r.at[phase, 1],
                (tm_next, lax.rem(tile + i, TILES)),
            ).start()
            return carry

        lax.fori_loop(1, TILES, to_group, 0)
        lax.fori_loop(0, TILES, to_next, 0)

    def exchange_wait(at_in, at_prev, phase, which):
        for i, ref in enumerate((at_in, at_prev)):
            copy = remote(ref, ref, stat_s.at[phase, i], stat_r.at[phase, i], partner)
            if which == "recv":
                copy.wait_recv()
            else:
                copy.wait_send()

    def halo_copies(ref, rim, phase):
        lo, hi = rim, rim + ROWS
        head, tail = (lo, lo + rim), (hi - rim, hi)
        cuts = [
            ((2, 6), head, (2, 6), (hi, hi + rim), (tm, up)),
            ((2, 6), tail, (2, 6), (0, rim), (tm, down)),
            ((4, 6), (lo, hi), (0, 2), (lo, hi), (tm_next, tile)),
            ((4, 6), head, (0, 2), (hi, hi + rim), (tm_next, up)),
            ((4, 6), tail, (0, 2), (0, rim), (tm_next, down)),
        ]
        return [
            remote(
                ref.at[a[0] : a[1], b[0] : b[1]], ref.at[c[0] : c[1], d[0] : d[1]],
                halo_s.at[phase, i], halo_r.at[phase, i], to,
            )
            for i, (a, b, c, d, to) in enumerate(cuts)
        ]

    pair = remote(fk_in, fk_pair, pair_s.at[0], pair_r.at[0], partner)
    pair.start()
    exchange(mine, st_in, st_prev, 0)
    halos = halo_copies(xraw, 1, 0)
    for copy in halos:
        copy.start()

    pair.wait_recv()
    odd = (core == 1).astype(F32)
    for t in range(27):
        a, b = fk_in[t].astype(F32), fk_pair[t].astype(F32)
        low, high = a + odd * (b - a), b + odd * (a - b)
        low = jnp.where(core == 1, b, a)
        high = jnp.where(core == 1, a, b)
        w1[t, z] = jnp.concatenate([low, high], axis=0).astype(BF16)

    my_x, my_y = 3 * x, XT + y
    spans = (("x", my_x, 3), ("y", my_y, 1), ("z", XT + YT, ZT))
    hops = 4

    def chip_of(k):
        return lax.rem(z - step * (k + 1) + 2 * NZ, NZ)

    def region(tap, count, chip):
        return w1.at[pl.ds(tap, count), chip]

    def z_copy(k, c):
        _, tap, count = spans[c]
        ref = region(tap, count, chip_of(k - 1))
        return remote(ref, ref, zs.at[k, c], zr.at[k, c], along_z(step))

    def x_tap(hop):
        by = (-step, -2 * step, step)[hop]
        return 3 * lax.rem(x + by + 2 * NX, NX)

    def x_copy(k, hop):
        tap = (my_x, x_tap(0), my_x)[hop]
        ref = region(tap, 3, chip_of(k))
        return remote(ref, ref, xs.at[k, hop], xr.at[k, hop], along_x((step, step, -step)[hop]))

    def y_tap(hop):
        by = -step * (hop + 1) if hop < 4 else step * (hop - 3)
        return XT + lax.rem(y + by + 2 * NY, NY)

    def y_copy(k, hop):
        tap = my_y if hop in (0, 4) else y_tap(hop - 1)
        ref = region(tap, 1, chip_of(k))
        return remote(ref, ref, ys.at[k, hop], yr.at[k, hop], along_y(step if hop < 4 else -step))

    parts = ((0, XT), (XT, YT), (XT + YT, ZT))

    def p_copy(k, c):
        ref = region(parts[c][0], parts[c][1], chip_of(k))
        return remote(ref, ref, ps.at[k, c], pr.at[k, c], partner)

    def block_guard(k, body):
        if k < hops - 1:
            body()
        else:
            pl.when(core == 0)(body)

    def z_stage(k):
        for c in (1, 0, 2):
            z_copy(k, c).wait_recv()
            if k + 1 < hops:
                block_guard(k + 1, lambda: z_copy(k + 1, c).start())
            if c == 0:
                x_copy(k, 0).start()
                x_copy(k, 2).start()
            elif c == 1:
                y_copy(k, 0).start()
                y_copy(k, 4).start()
            else:
                p_copy(k, 2).start()

    def xy_first(k):
        x_copy(k, 0).wait_recv()
        x_copy(k, 1).start()
        x_copy(k, 2).wait_recv()
        y_copy(k, 0).wait_recv()
        y_copy(k, 1).start()
        y_copy(k, 4).wait_recv()
        y_copy(k, 5).start()

    def xy_second(k):
        x_copy(k, 1).wait_recv()
        p_copy(k, 0).start()
        y_copy(k, 1).wait_recv()
        y_copy(k, 2).start()
        y_copy(k, 5).wait_recv()
        y_copy(k, 6).start()

    def y_third(k):
        y_copy(k, 2).wait_recv()
        y_copy(k, 3).start()
        y_copy(k, 6).wait_recv()

    def y_fourth(k):
        y_copy(k, 3).wait_recv()
        p_copy(k, 1).start()

    stages = (z_stage, xy_first, xy_second, y_third, y_fourth)

    def wave(s):
        for depth, stage in enumerate(stages):
            k = s - depth
            if 0 <= k < hops:
                block_guard(k, functools.partial(stage, k))

    for c in (1, 0, 2):
        z_copy(0, c).start()

    loads[4].wait()
    for a in range(2):
        for tap in range(2):
            if a == 0:
                q = [rkv[0, d].astype(F32) for d in range(3)] if tap == 0 else [
                    rkv[1, d].astype(F32) + rkv[2, d].astype(F32) for d in range(3)
                ]
            else:
                q = [rkv[0, d].astype(F32) + rkv[1, d].astype(F32) for d in range(3)] if tap == 0 else [
                    rkv[2, d].astype(F32) for d in range(3)
                ]
            none = jnp.zeros_like(q[0])
            cols = [
                jnp.concatenate([q[0], none], axis=1),
                jnp.concatenate([q[1] + q[2], q[0] + q[1]], axis=1),
                jnp.concatenate([none, q[2]], axis=1),
            ]
            for d in range(3):
                wres[a, (tap * 3 + d) * CMID : (tap * 3 + d + 1) * CMID, :] = cols[d].astype(BF16)

    total = clips[0] * 0
    starts_here = span_start(clips, tm)
    keep_prev = jnp.where(starts_here, 0.0, 1.0).astype(F32)
    keep_top = jnp.where(tile == 0, 0.0, 1.0).astype(F32)
    keep_bottom = jnp.where(tile == TILES - 1, 0.0, 1.0).astype(F32)

    exchange_wait(st_in, st_prev, 0, "recv")
    total = jnp.sum(st_in[...], axis=0) + mine[...]
    total_prev = jnp.sum(st_prev[...], axis=0)
    own, prev = affine(total, total_prev, g1[...], b1[...], CIN // GROUPS)
    for copy in halos:
        copy.wait_recv()
    for f in range(6):
        scale, shift = (own[0][f - 2], own[1][f - 2]) if f >= 2 else (prev[0][f + 2], prev[1][f + 2])
        v = xraw[f].astype(F32) * scale[None, None, :] + shift[None, None, :]
        a = silu(v)
        if f < 2:
            a = a * keep_prev
        a = jnp.concatenate([a[0:1] * keep_top, a[1:5], a[5:6] * keep_bottom], axis=0)
        for d, part in enumerate(shifted(a)):
            x1[f, :, :, d * CIN : (d + 1) * CIN] = part.astype(BF16)

    for s in range(hops + len(stages) - 1):
        wave(s)

    def partner_wait(c):
        for k in range(hops):
            ref = region(parts[c][0], parts[c][1], 0)
            copy = remote(ref, ref, ps.at[k, c], pr.at[k, c], partner)
            if k < hops - 1:
                copy.wait_recv()
            else:
                pl.when(core == 1)(copy.wait_recv)

    def conv1(groups, first):
        total = None if first else acc_ref[...]
        for g in groups:
            s, dy = divmod(g, 3)
            window = x1[s : s + FR, dy : dy + ROWS].reshape(FR * ROWS * COLS, 3 * CIN)
            weights = w1[3 * g : 3 * g + 3].reshape(3 * CIN, CMID)
            term = jnp.dot(window, weights, preferred_element_type=F32)
            total = term if total is None else total + term
        acc_ref[...] = total

    partner_wait(2)
    conv1((7, 8), True)
    partner_wait(0)
    conv1((0, 1, 2, 3), False)
    partner_wait(1)
    conv1((4, 5, 6), False)

    hidden = acc_ref[...].reshape(FR, ROWS * COLS, CMID)
    hown[...] = hidden.reshape(FR, ROWS, COLS, CMID)
    hraw[2:6, 2:6] = hidden.reshape(FR, ROWS, COLS, CMID).astype(BF16)
    halos2 = halo_copies(hraw, 2, 1)
    for copy in halos2:
        copy.start()
    mine2[...] = partial_stats(jnp.sum(hidden, axis=1), jnp.sum(hidden * hidden, axis=1), CMID // GROUPS)
    exchange(mine2, st_in2, st_prev2, 1)

    loads[3].wait()
    loads[2].wait()
    shortcut = lax.dot_general(
        xraw[2:6].reshape(FR * 6 * COLS, CIN), wskip[...], (((1,), (1,)), ((), ())),
        preferred_element_type=F32,
    )

    exchange_wait(st_in2, st_prev2, 1, "recv")
    total = jnp.sum(st_in2[...], axis=0) + mine2[...]
    total_prev = jnp.sum(st_prev2[...], axis=0)
    own, prev = affine(total, total_prev, g2[...], b2[...], CMID // GROUPS)
    for copy in halos2:
        copy.wait_recv()
    for f in range(6):
        scale, shift = (own[0][f - 2], own[1][f - 2]) if f >= 2 else (prev[0][f + 2], prev[1][f + 2])
        if f >= 2:
            v = jnp.concatenate(
                [hraw[f, 0:2].astype(F32), hown[f - 2], hraw[f, 6:8].astype(F32)], axis=0
            )
        else:
            v = hraw[f].astype(F32)
        a = silu(v * scale[None, None, :] + shift[None, None, :])
        if f < 2:
            a = a * keep_prev
        a = jnp.concatenate([a[0:2] * keep_top, a[2:6], a[6:8] * keep_bottom], axis=0)
        x2[f] = jnp.concatenate(shifted(a), axis=-1).astype(BF16)

    total = shortcut
    for g in range(9):
        s, dy = divmod(g, 3)
        window = x2[s : s + FR, dy : dy + 6].reshape(FR * 6 * COLS, 3 * CMID)
        weights = w2[3 * g : 3 * g + 3].reshape(3 * CMID, CMID)
        total = total + jnp.dot(window, weights, preferred_element_type=F32)
    block = total.astype(BF16).astype(F32).reshape(FR, 6, COLS, CMID)
    for f in range(FR):
        a = jnp.concatenate(
            [block[f, 0:1] * keep_top, block[f, 1:5], block[f, 5:6] * keep_bottom], axis=0
        )
        x3[f] = jnp.concatenate(shifted(a), axis=-1).astype(BF16)

    for a in range(2):
        window = jnp.concatenate(
            [x3[:, a : a + ROWS], x3[:, a + 1 : a + 1 + ROWS]], axis=-1
        ).reshape(FR * ROWS * COLS, 6 * CMID)
        res = jnp.dot(window, wres[a], preferred_element_type=F32)
        res = res.astype(BF16).reshape(FR, ROWS, COLS, 2 * COUT)
        out_v[:, :, a] = res
    store = pltpu.make_async_copy(out_v, out, load_sem.at[5])
    store.start()

    pair.wait_send()
    for copy in halos + halos2:
        copy.wait_send()
    exchange_wait(st_in, st_prev, 0, "send")
    exchange_wait(st_in2, st_prev2, 1, "send")

    def drain(k):
        for c in range(3):
            z_copy(k, c).wait_send()
            p_copy(k, c).wait_send()
            x_copy(k, c).wait_send()
        for hop in range(7):
            y_copy(k, hop).wait_send()

    for k in range(hops):
        block_guard(k, functools.partial(drain, k))
    store.wait()


def span_start(clips, tm):
    start, hit = jnp.int32(0), tm == 0
    for j in range(3):
        start = start + clips[j]
        hit = hit | (start == tm)
    return hit


def shards(
    latents, first_gain, first_bias, first_kernel, second_gain, second_bias,
    second_kernel, skip_weight, resample_kernel, clip_spans,
):
    fk = jnp.transpose(first_kernel, (1, 2, 3, 0, 4)).reshape(27, SHARD, CMID)
    sk = jnp.transpose(second_kernel, (1, 2, 3, 0, 4)).reshape(27, CMID, CMID)
    anywhere = pl.BlockSpec(memory_space=pl.ANY)
    vmem = pl.BlockSpec(memory_space=pltpu.VMEM)
    smem = pl.BlockSpec(memory_space=pltpu.SMEM)
    dma = pltpu.SemaphoreType.DMA
    out = pl.pallas_call(
        kernel,
        out_shape=jax.ShapeDtypeStruct((FR, ROWS, 2, COLS, 2 * COUT), BF16),
        in_specs=[anywhere, vmem, vmem, anywhere, vmem, vmem, anywhere, anywhere, anywhere, smem],
        out_specs=anywhere,
        scratch_shapes=[
            pltpu.VMEM((6, 6, COLS, CIN), BF16),
            pltpu.VMEM((27, SHARD, CMID), BF16),
            pltpu.VMEM((27, SHARD, CMID), BF16),
            pltpu.VMEM((27, NZ, UNIT, CMID), BF16),
            pltpu.VMEM((27, CMID, CMID), BF16),
            pltpu.VMEM((CMID, CIN), BF16),
            pltpu.VMEM((3, 3, CMID, COUT), BF16),
            pltpu.VMEM((6, 6, COLS, 3 * CIN), BF16),
            pltpu.VMEM((FR, ROWS, COLS, CMID), F32),
            pltpu.VMEM((6, 8, COLS, CMID), BF16),
            pltpu.VMEM((6, 8, COLS, 3 * CMID), BF16),
            pltpu.VMEM((FR, 6, COLS, 3 * CMID), BF16),
            pltpu.VMEM((2, 6 * CMID, 2 * COUT), BF16),
            pltpu.VMEM((FR * ROWS * COLS, CMID), F32),
            pltpu.VMEM((FR, ROWS, 2, COLS, 2 * COUT), BF16),
            pltpu.VMEM((2, 128), F32),
            pltpu.VMEM((TILES - 1, 2, 128), F32),
            pltpu.VMEM((TILES, 2, 128), F32),
            pltpu.VMEM((2, 128), F32),
            pltpu.VMEM((TILES - 1, 2, 128), F32),
            pltpu.VMEM((TILES, 2, 128), F32),
            dma((6,)),
            dma((2, 5)), dma((2, 5)),
            dma((2, 2)), dma((2, 2)),
            dma((1,)), dma((1,)),
            dma((4, 3)), dma((4, 3)),
            dma((4, 3)), dma((4, 3)),
            dma((4, 7)), dma((4, 7)),
            dma((4, 3)), dma((4, 3)),
        ],
        compiler_params=pltpu.CompilerParams(
            collective_id=0, has_side_effects=True, vmem_limit_bytes=56 * 2**20
        ),
    )(
        latents, first_gain.reshape(1, CIN), first_bias.reshape(1, CIN), fk,
        second_gain.reshape(1, CMID), second_bias.reshape(1, CMID), sk, skip_weight.T,
        resample_kernel, clip_spans,
    )
    return out.reshape(FR, 2 * ROWS, COLS, 2 * COUT)


def solution(mesh):
    in_specs = (
        P("tm", "tile", None, None), P(), P(), P("tile", None, None, None, None),
        P(), P(), P(), P(), P(), P(),
    )
    return jax.shard_map(
        shards, mesh=mesh, in_specs=in_specs, out_specs=P("tm", "tile", None, None), check_vma=False
    )
```

time: 170 us -> 70.7 us (0.42)
  the two profiles are of different devices: /device:TPU:225 before, /device:TPU:1 now
where the time goes in v1:
time: 70.7 us; the launch traced here: 70.5 us
  Pallas kernels  66.3 us (94%)
  local copies, waits for them, and re-layouts  4.17 us (6%)
    pallas_call x1, Pallas kernels, shards(): pl.pallas_call(kernel, out_shape=jax.ShapeDtypeStruct((FR, ROWS, 2, COLS,...  66.3 us
    unnamed x1, local copies, waits for them, and re-layouts  1.67 us

profile of v1, /device:TPU:1, one launch (start us, length us, event | category | flops | bytes accessed | tf_op | source)
XLA Modules:
  0.0 70.5 jit_solution(1913305671000046006)
XLA Ops:
  0.0 1.2 %reshape.21.g1 = f32[1,384]{1,0:T(1,128)} reshape(f32[384]{0:T(512)} %param.11) | data formatting | bytes 3072 | tf_op jit(solution)/shard_map/reshape | solution.py:517
  1.2 1.3 %reshape.22.b1 = f32[1,384]{1,0:T(1,128)} reshape(f32[384]{0:T(512)} %param.12) | data formatting | bytes 3072 | tf_op jit(solution)/shard_map/reshape | solution.py:517
  2.5 66.3 %shard_map.100 = bf16[4,4,2,16,192]{4,3,2,1,0:T(8,128)(2,1)} custom-call(bf16[4,4,16,384]{3,2,1,0:T(8,128)(2,1)} %lat.1, f32[1,384]{1,0:T(1,128)} %reshape.21.g1, f32[1,384]{1,0:T(1,128)} %reshape.22.b1, bf16[27,24,192]{2,1,0:T(8,128)(2,1)} %bitcast.12, f32[1,192]{1,0:T(1,128)} %bitcast.14, f32[1,192]{1,0:T(1,128)} %bitcast.15, ...), custom_call_target="tpu_custom_call" | custom-call | tf_op jit(solution)/shard_map/pallas_call | solution.py:477
  68.8 1.7 %copy.12 = bf16[4,8,16,192]{3,2,1,0:T(8,128)(2,1)} copy(bf16[4,8,16,192]{3,2,1,0:T(8,128)(2,1)} %bitcast.11) | data formatting | bytes 393216

commit v2 on v1

--- a/solution.py
+++ b/solution.py
@@ -19,8 +19,10 @@
 NX, NY, NZ = 4, 8, 8
 SHARD = CIN // TILES
 UNIT = 2 * SHARD
-XT, YT = 12, 8
-ZT = 27 - XT - YT
+UNITS = 41
+XU, YU = 6, 2
+XT, YT = XU * NX, YU * NY
+ZT = UNITS - XT - YT
 HEIGHT = ROWS * TILES
 
 
@@ -82,7 +84,7 @@
 def kernel(
     lat, g1, b1, fk, g2, b2, sk, skw, rk, clips, out,
     xraw, fk_in, fk_pair, w1, w2, wskip, rkv, x1, hown, hraw, x2, x3, wres, acc_ref, out_v,
-    mine, st_in, st_prev, mine2, st_in2, st_prev2,
+    mine, st_in, st_total, st_prev, mine2, st_in2, st_total2, st_prev2,
     load_sem, halo_s, halo_r, stat_s, stat_r, pair_s, pair_r,
     zs, zr, xs, xr, ys, yr, ps, pr,
 ):
@@ -121,6 +123,8 @@
         load.start()
 
     barrier = pltpu.get_barrier_semaphore()
+    near = [along_x(1), along_x(-1), along_y(1), along_y(-1), along_y(2), along_y(-2)]
+    near += [(tm_prev, tile), (tm_prev, up), (tm_prev, down)]
 
     def greet(to):
         pl.semaphore_signal(barrier, inc=1, device_id=to, device_id_type=pl.DeviceIdType.MESH)
@@ -129,17 +133,9 @@
         greet((tm, lax.rem(tile + i, TILES)))
         return carry
 
-    def greet_prev(i, carry):
-        greet((tm_prev, lax.rem(tile + i, TILES)))
-        return carry
-
     lax.fori_loop(1, TILES, greet_group, 0)
-    lax.fori_loop(0, TILES, greet_prev, 0)
-    x_steps = (1, -1)
-    for by in x_steps:
-        greet(along_x(by))
-    for by in x_steps:
-        greet(along_y(by))
+    for to in near:
+        greet(to)
 
     loads[0].wait()
     sums, squares = [], []
@@ -149,9 +145,9 @@
         squares.append(jnp.sum(v * v, axis=0, keepdims=True))
     mine[...] = partial_stats(jnp.concatenate(sums), jnp.concatenate(squares), CIN // GROUPS)
     loads[1].wait()
-    pl.semaphore_wait(barrier, TILES - 1 + TILES + 4)
-
-    def exchange(src, at_in, at_prev, phase):
+    pl.semaphore_wait(barrier, TILES - 1 + len(near))
+
+    def exchange(src, at_in, phase):
         def to_group(i, carry):
             remote(
                 src, at_in.at[i - 1], stat_s.at[phase, 0], stat_r.at[phase, 0],
@@ -159,23 +155,13 @@
             ).start()
             return carry
 
-        def to_next(i, carry):
-            remote(
-                src, at_prev.at[i], stat_s.at[phase, 1], stat_r.at[phase, 1],
-                (tm_next, lax.rem(tile + i, TILES)),
-            ).start()
-            return carry
-
         lax.fori_loop(1, TILES, to_group, 0)
-        lax.fori_loop(0, TILES, to_next, 0)
-
-    def exchange_wait(at_in, at_prev, phase, which):
-        for i, ref in enumerate((at_in, at_prev)):
-            copy = remote(ref, ref, stat_s.at[phase, i], stat_r.at[phase, i], partner)
-            if which == "recv":
-                copy.wait_recv()
-            else:
-                copy.wait_send()
+
+    def exchange_copy(at_in, phase):
+        return remote(at_in, at_in, stat_s.at[phase, 0], stat_r.at[phase, 0], partner)
+
+    def relay(total, at_prev, phase):
+        return remote(total, at_prev, stat_s.at[phase, 1], stat_r.at[phase, 1], (tm_next, tile))
 
     def halo_copies(ref, rim, phase):
         lo, hi = rim, rim + ROWS
@@ -197,52 +183,58 @@
 
     pair = remote(fk_in, fk_pair, pair_s.at[0], pair_r.at[0], partner)
     pair.start()
-    exchange(mine, st_in, st_prev, 0)
+    exchange(mine, st_in, 0)
     halos = halo_copies(xraw, 1, 0)
     for copy in halos:
         copy.start()
 
     pair.wait_recv()
-    odd = (core == 1).astype(F32)
-    for t in range(27):
+
+    def both_halves(t):
         a, b = fk_in[t].astype(F32), fk_pair[t].astype(F32)
-        low, high = a + odd * (b - a), b + odd * (a - b)
-        low = jnp.where(core == 1, b, a)
-        high = jnp.where(core == 1, a, b)
-        w1[t, z] = jnp.concatenate([low, high], axis=0).astype(BF16)
-
-    my_x, my_y = 3 * x, XT + y
-    spans = (("x", my_x, 3), ("y", my_y, 1), ("z", XT + YT, ZT))
+        return jnp.concatenate([jnp.where(core == 1, b, a), jnp.where(core == 1, a, b)], axis=0)
+
+    for p in range(14):
+        even = both_halves(2 * p)
+        w1[3 * p, z] = even[:, :128].astype(BF16)
+        if p < 13:
+            odd = both_halves(2 * p + 1)
+            w1[3 * p + 1, z] = odd[:, :128].astype(BF16)
+            rest = jnp.concatenate([even[:, 128:], odd[:, 128:]], axis=1)
+            w1[3 * p + 2, z] = rest.astype(BF16)
+        else:
+            rest = jnp.concatenate([even[:, 128:], jnp.zeros_like(even[:, 128:])], axis=1)
+            w1[3 * p + 1, z] = rest.astype(BF16)
+
+    my_x, my_y = XU * x, XT + YU * y
+    spans = ((my_x, XU), (my_y, YU), (XT + YT, ZT))
     hops = 4
 
     def chip_of(k):
         return lax.rem(z - step * (k + 1) + 2 * NZ, NZ)
 
-    def region(tap, count, chip):
-        return w1.at[pl.ds(tap, count), chip]
+    def region(unit, count, chip):
+        return w1.at[pl.ds(unit, count), chip]
 
     def z_copy(k, c):
-        _, tap, count = spans[c]
-        ref = region(tap, count, chip_of(k - 1))
-        return remote(ref, ref, zs.at[k, c], zr.at[k, c], along_z(step))
-
-    def x_tap(hop):
-        by = (-step, -2 * step, step)[hop]
-        return 3 * lax.rem(x + by + 2 * NX, NX)
+        unit, count = spans[c]
+        if c == 1 or k < 2:
+            ref, by = region(unit, count, z), step * (k + 1)
+        else:
+            ref, by = region(unit, count, chip_of(1)), step * (k - 1)
+        return remote(ref, ref, zs.at[k, c], zr.at[k, c], along_z(by))
 
     def x_copy(k, hop):
-        tap = (my_x, x_tap(0), my_x)[hop]
-        ref = region(tap, 3, chip_of(k))
+        unit = my_x if hop != 1 else XU * lax.rem(x - step + NX, NX)
+        ref = region(unit, XU, chip_of(k))
         return remote(ref, ref, xs.at[k, hop], xr.at[k, hop], along_x((step, step, -step)[hop]))
 
-    def y_tap(hop):
-        by = -step * (hop + 1) if hop < 4 else step * (hop - 3)
-        return XT + lax.rem(y + by + 2 * NY, NY)
-
     def y_copy(k, hop):
-        tap = my_y if hop in (0, 4) else y_tap(hop - 1)
-        ref = region(tap, 1, chip_of(k))
-        return remote(ref, ref, ys.at[k, hop], yr.at[k, hop], along_y(step if hop < 4 else -step))
+        origin = {2: -2 * step, 3: -2 * step, 6: 2 * step}.get(hop, 0)
+        by = (step, 2 * step, step, 2 * step, -step, -2 * step, -step)[hop]
+        unit = XT + YU * lax.rem(y + origin + NY, NY)
+        ref = region(unit, YU, chip_of(k))
+        return remote(ref, ref, ys.at[k, hop], yr.at[k, hop], along_y(by))
 
     parts = ((0, XT), (XT, YT), (XT + YT, ZT))
 
@@ -256,56 +248,60 @@
         else:
             pl.when(core == 0)(body)
 
-    def z_stage(k):
-        for c in (1, 0, 2):
-            z_copy(k, c).wait_recv()
-            if k + 1 < hops:
-                block_guard(k + 1, lambda: z_copy(k + 1, c).start())
-            if c == 0:
-                x_copy(k, 0).start()
-                x_copy(k, 2).start()
-            elif c == 1:
-                y_copy(k, 0).start()
-                y_copy(k, 4).start()
-            else:
-                p_copy(k, 2).start()
-
-    def xy_first(k):
-        x_copy(k, 0).wait_recv()
-        x_copy(k, 1).start()
-        x_copy(k, 2).wait_recv()
-        y_copy(k, 0).wait_recv()
-        y_copy(k, 1).start()
-        y_copy(k, 4).wait_recv()
-        y_copy(k, 5).start()
-
-    def xy_second(k):
-        x_copy(k, 1).wait_recv()
-        p_copy(k, 0).start()
+    def z_start():
+        for k in (3, 2, 1, 0):
+            block_guard(k, lambda: z_copy(k, 1).start())
+        for k in (0, 1):
+            z_copy(k, 0).start()
+        for k in (0, 1):
+            z_copy(k, 2).start()
+
+    def zy_arrived(k):
+        z_copy(k, 1).wait_recv()
+        for hop in (1, 5, 0, 4):
+            y_copy(k, hop).start()
+
+    def zx_arrived(k):
+        z_copy(k, 0).wait_recv()
+        if k == 1:
+            z_copy(2, 0).start()
+            block_guard(3, lambda: z_copy(3, 0).start())
+        x_copy(k, 0).start()
+        x_copy(k, 2).start()
+
+    def zz_arrived(k):
+        z_copy(k, 2).wait_recv()
+        if k == 1:
+            z_copy(2, 2).start()
+            block_guard(3, lambda: z_copy(3, 2).start())
+        p_copy(k, 2).start()
+
+    def y_near(k):
         y_copy(k, 1).wait_recv()
+        y_copy(k, 3).start()
         y_copy(k, 2).start()
         y_copy(k, 5).wait_recv()
         y_copy(k, 6).start()
 
-    def y_third(k):
-        y_copy(k, 2).wait_recv()
-        y_copy(k, 3).start()
-        y_copy(k, 6).wait_recv()
-
-    def y_fourth(k):
-        y_copy(k, 3).wait_recv()
+    def y_rest(k):
+        for hop in (0, 4, 2, 6, 3):
+            y_copy(k, hop).wait_recv()
         p_copy(k, 1).start()
 
-    stages = (z_stage, xy_first, xy_second, y_third, y_fourth)
-
-    def wave(s):
-        for depth, stage in enumerate(stages):
-            k = s - depth
-            if 0 <= k < hops:
-                block_guard(k, functools.partial(stage, k))
-
-    for c in (1, 0, 2):
-        z_copy(0, c).start()
+    def x_near(k):
+        x_copy(k, 0).wait_recv()
+        x_copy(k, 1).start()
+
+    def x_rest(k):
+        x_copy(k, 2).wait_recv()
+        x_copy(k, 1).wait_recv()
+        p_copy(k, 0).start()
+
+    def run(stage, *blocks):
+        for k in blocks:
+            block_guard(k, functools.partial(stage, k))
+
+    z_start()
 
     loads[4].wait()
     for a in range(2):
@@ -327,16 +323,21 @@
             for d in range(3):
                 wres[a, (tap * 3 + d) * CMID : (tap * 3 + d + 1) * CMID, :] = cols[d].astype(BF16)
 
-    total = clips[0] * 0
     starts_here = span_start(clips, tm)
     keep_prev = jnp.where(starts_here, 0.0, 1.0).astype(F32)
     keep_top = jnp.where(tile == 0, 0.0, 1.0).astype(F32)
     keep_bottom = jnp.where(tile == TILES - 1, 0.0, 1.0).astype(F32)
 
-    exchange_wait(st_in, st_prev, 0, "recv")
-    total = jnp.sum(st_in[...], axis=0) + mine[...]
-    total_prev = jnp.sum(st_prev[...], axis=0)
-    own, prev = affine(total, total_prev, g1[...], b1[...], CIN // GROUPS)
+    exchange_copy(st_in, 0).wait_recv()
+    st_total[...] = jnp.sum(st_in[...], axis=0) + mine[...]
+    relayed = relay(st_total, st_prev, 0)
+    relayed.start()
+    run(zy_arrived, 0, 1, 2, 3)
+    run(zx_arrived, 0, 1)
+    relayed.wait_recv()
+    own, prev = affine(
+        st_total[...], st_prev[...], g1[...].reshape(1, CIN), b1[...].reshape(1, CIN), CIN // GROUPS
+    )
     for copy in halos:
         copy.wait_recv()
     for f in range(6):
@@ -349,8 +350,14 @@
         for d, part in enumerate(shifted(a)):
             x1[f, :, :, d * CIN : (d + 1) * CIN] = part.astype(BF16)
 
-    for s in range(hops + len(stages) - 1):
-        wave(s)
+    run(y_near, 0, 1, 2, 3)
+    run(x_near, 0, 1)
+    run(zx_arrived, 2, 3)
+    run(zz_arrived, 0, 1, 2, 3)
+    run(x_rest, 0, 1)
+    run(y_rest, 0, 1, 2, 3)
+    run(x_near, 2, 3)
+    run(x_rest, 2, 3)
 
     def partner_wait(c):
         for k in range(hops):
@@ -361,31 +368,38 @@
             else:
                 pl.when(core == 1)(copy.wait_recv)
 
-    def conv1(groups, first):
-        total = None if first else acc_ref[...]
-        for g in groups:
-            s, dy = divmod(g, 3)
-            window = x1[s : s + FR, dy : dy + ROWS].reshape(FR * ROWS * COLS, 3 * CIN)
-            weights = w1[3 * g : 3 * g + 3].reshape(3 * CIN, CMID)
-            term = jnp.dot(window, weights, preferred_element_type=F32)
-            total = term if total is None else total + term
-        acc_ref[...] = total
-
+    def tap_window(t):
+        s, rest = divmod(t, 9)
+        dy, dx = divmod(rest, 3)
+        window = x1[s : s + FR, dy : dy + ROWS, :, dx * CIN : (dx + 1) * CIN]
+        return window.reshape(FR * ROWS * COLS, CIN)
+
+    def conv1(pairs, first):
+        total = [None, None] if first else [acc_ref[0], acc_ref[1]]
+        for p in pairs:
+            rest = w1[3 * p + (2 if p < 13 else 1)].reshape(CIN, 128)
+            for odd in range(2 if p < 13 else 1):
+                weights = jnp.concatenate([w1[3 * p + odd].reshape(CIN, 128), rest], axis=1)
+                term = jnp.dot(tap_window(2 * p + odd), weights, preferred_element_type=F32)
+                total[odd] = term if total[odd] is None else total[odd] + term
+        acc_ref[0], acc_ref[1] = total
+
+    partner_wait(1)
     partner_wait(2)
-    conv1((7, 8), True)
+    conv1(range(8, 14), True)
     partner_wait(0)
-    conv1((0, 1, 2, 3), False)
-    partner_wait(1)
-    conv1((4, 5, 6), False)
-
-    hidden = acc_ref[...].reshape(FR, ROWS * COLS, CMID)
+    conv1(range(0, 8), False)
+
+    even, odd = acc_ref[0], acc_ref[1]
+    hidden = jnp.concatenate([even[:, :128] + odd[:, :128], even[:, 128:192] + odd[:, 192:]], axis=1)
+    hidden = hidden.reshape(FR, ROWS * COLS, CMID)
     hown[...] = hidden.reshape(FR, ROWS, COLS, CMID)
     hraw[2:6, 2:6] = hidden.reshape(FR, ROWS, COLS, CMID).astype(BF16)
     halos2 = halo_copies(hraw, 2, 1)
     for copy in halos2:
         copy.start()
     mine2[...] = partial_stats(jnp.sum(hidden, axis=1), jnp.sum(hidden * hidden, axis=1), CMID // GROUPS)
-    exchange(mine2, st_in2, st_prev2, 1)
+    exchange(mine2, st_in2, 1)
 
     loads[3].wait()
     loads[2].wait()
@@ -394,10 +408,14 @@
         preferred_element_type=F32,
     )
 
-    exchange_wait(st_in2, st_prev2, 1, "recv")
-    total = jnp.sum(st_in2[...], axis=0) + mine2[...]
-    total_prev = jnp.sum(st_prev2[...], axis=0)
-    own, prev = affine(total, total_prev, g2[...], b2[...], CMID // GROUPS)
+    exchange_copy(st_in2, 1).wait_recv()
+    st_total2[...] = jnp.sum(st_in2[...], axis=0) + mine2[...]
+    relayed2 = relay(st_total2, st_prev2, 1)
+    relayed2.start()
+    relayed2.wait_recv()
+    own, prev = affine(
+        st_total2[...], st_prev2[...], g2[...].reshape(1, CMID), b2[...].reshape(1, CMID), CMID // GROUPS
+    )
     for copy in halos2:
         copy.wait_recv()
     for f in range(6):
@@ -440,8 +458,8 @@
     pair.wait_send()
     for copy in halos + halos2:
         copy.wait_send()
-    exchange_wait(st_in, st_prev, 0, "send")
-    exchange_wait(st_in2, st_prev2, 1, "send")
+    for copy in (exchange_copy(st_in, 0), exchange_copy(st_in2, 1), relayed, relayed2):
+        copy.wait_send()
 
     def drain(k):
         for c in range(3):
@@ -483,7 +501,7 @@
             pltpu.VMEM((6, 6, COLS, CIN), BF16),
             pltpu.VMEM((27, SHARD, CMID), BF16),
             pltpu.VMEM((27, SHARD, CMID), BF16),
-            pltpu.VMEM((27, NZ, UNIT, CMID), BF16),
+            pltpu.VMEM((UNITS, NZ, UNIT, 128), BF16),
             pltpu.VMEM((27, CMID, CMID), BF16),
             pltpu.VMEM((CMID, CIN), BF16),
             pltpu.VMEM((3, 3, CMID, COUT), BF16),
@@ -493,14 +511,16 @@
             pltpu.VMEM((6, 8, COLS, 3 * CMID), BF16),
             pltpu.VMEM((FR, 6, COLS, 3 * CMID), BF16),
             pltpu.VMEM((2, 6 * CMID, 2 * COUT), BF16),
-            pltpu.VMEM((FR * ROWS * COLS, CMID), F32),
+            pltpu.VMEM((2, FR * ROWS * COLS, 256), F32),
             pltpu.VMEM((FR, ROWS, 2, COLS, 2 * COUT), BF16),
             pltpu.VMEM((2, 128), F32),
             pltpu.VMEM((TILES - 1, 2, 128), F32),
-            pltpu.VMEM((TILES, 2, 128), F32),
+            pltpu.VMEM((2, 128), F32),
+            pltpu.VMEM((2, 128), F32),
             pltpu.VMEM((2, 128), F32),
             pltpu.VMEM((TILES - 1, 2, 128), F32),
-            pltpu.VMEM((TILES, 2, 128), F32),
+            pltpu.VMEM((2, 128), F32),
+            pltpu.VMEM((2, 128), F32),
             dma((6,)),
             dma((2, 5)), dma((2, 5)),
             dma((2, 2)), dma((2, 2)),
@@ -514,8 +534,8 @@
             collective_id=0, has_side_effects=True, vmem_limit_bytes=56 * 2**20
         ),
     )(
-        latents, first_gain.reshape(1, CIN), first_bias.reshape(1, CIN), fk,
-        second_gain.reshape(1, CMID), second_bias.reshape(1, CMID), sk, skip_weight.T,
+        latents, first_gain, first_bias, fk,
+        second_gain, second_bias, sk, skip_weight.T,
         resample_kernel, clip_spans,
     )
     return out.reshape(FR, 2 * ROWS, COLS, 2 * COUT)

time: 70.7 us -> 57.3 us (0.81); the launches traced: 70.5 us -> 56.3 us
  Pallas kernels: 66.3 us -> 54.6 us
  local copies, waits for them, and re-layouts: 4.17 us -> 1.67 us
    pallas_call x1, Pallas kernels: 66.3 us -> 54.6 us  [shards(): pl.pallas_call(kernel, out_shape=jax.ShapeDtypeStruct((FR, ROWS, 2, COLS,...]
    reshape x2 -> x0, local copies, waits for them, and re-layouts: 2.5 us -> none  [the longest x1 1.25 us: shards(): first_bias.reshape(1, CIN)]
where the time goes in v2:
time: 57.3 us; the launch traced here: 56.3 us
  Pallas kernels  54.6 us (95%)
  local copies, waits for them, and re-layouts  1.67 us (3%)
    pallas_call x1, Pallas kernels, shards(): pl.pallas_call(kernel, out_shape=jax.ShapeDtypeStruct((FR, ROWS, 2, COLS,...  54.6 us
    unnamed x1, local copies, waits for them, and re-layouts  1.67 us

profile of v2, /device:TPU:1, one launch (start us, length us, event | category | flops | bytes accessed | tf_op | source)
XLA Modules:
  0.0 56.3 jit_solution(6240850809202805512)
XLA Ops:
  0.0 54.6 %shard_map.100 = bf16[4,4,2,16,192]{4,3,2,1,0:T(8,128)(2,1)} custom-call(bf16[4,4,16,384]{3,2,1,0:T(8,128)(2,1)} %lat.1, f32[384]{0:T(512)} %g1.1, f32[384]{0:T(512)} %b1.1, bf16[27,24,192]{2,1,0:T(8,128)(2,1)} %bitcast.10, f32[192]{0:T(256)} %g2.1, f32[192]{0:T(256)} %b2.1, bf16[27,192,192]{2,1,0:T(8,128)(2,1)} %bitcast.8, bf16[192,384]{1,0:T(8,128)(2,1)} %bitcast.11, ...), custom_call_target="tpu_custom_call" | custom-call | tf_op jit(solution)/shard_map/pallas_call | solution.py:495
  54.6 1.7 %copy.12 = bf16[4,8,16,192]{3,2,1,0:T(8,128)(2,1)} copy(bf16[4,8,16,192]{3,2,1,0:T(8,128)(2,1)} %bitcast.9) | data formatting | bytes 393216

commit v3 on v2

v3 whole, which is shorter than its diff:
```python
import functools

import jax
import jax.numpy as jnp
from jax import lax
from jax.experimental import pallas as pl
from jax.experimental.pallas import tpu as pltpu
from jax.sharding import PartitionSpec as P

GROUPS = 32
EPS = 1e-6
F32 = jnp.float32
BF16 = jnp.bfloat16

FR, ROWS, COLS = 4, 4, 16
CIN, CMID, COUT = 384, 192, 96
SPANS, TILES = 32, 16
NX, NY, NZ = 4, 8, 8
SHARD = CIN // TILES
UNIT = 2 * SHARD
UNITS = 41
XU = 8
XT = XU * NX
ZT = UNITS - XT
HEIGHT = ROWS * TILES


def member(per, transposed):
    channels = per * GROUPS
    shape = (128, channels) if transposed else (channels, 128)
    lane = lax.broadcasted_iota(jnp.int32, shape, 0 if transposed else 1)
    chan = lax.broadcasted_iota(jnp.int32, shape, 1 if transposed else 0)
    first = jnp.bitwise_and(lane, GROUPS - 1) * per
    return jnp.where((chan >= first) & (chan < first + per), 1.0, 0.0).astype(BF16)


def frame_lanes(rows):
    lane = lax.broadcasted_iota(jnp.int32, (rows, 128), 1)
    row = lax.broadcasted_iota(jnp.int32, (rows, 128), 0)
    low = jnp.bitwise_and(row, FR - 1) * GROUPS
    return (lane >= low) & (lane < low + GROUPS)


def exact_dot(values, zero_one):
    rows = values.shape[0]
    high = values.astype(BF16).astype(F32)
    left = values - high
    middle = left.astype(BF16).astype(F32)
    terms = jnp.concatenate([high, middle, left - middle], axis=0).astype(BF16)
    wide = jnp.dot(terms, zero_one, preferred_element_type=F32)
    return wide[:rows] + wide[rows : 2 * rows] + wide[2 * rows :]


def partial_stats(sums, squares, to_lanes):
    wide = exact_dot(jnp.concatenate([sums, squares], axis=0), to_lanes)
    wide = jnp.where(frame_lanes(2 * FR), wide, 0.0)
    return jnp.concatenate(
        [jnp.sum(wide[:FR], axis=0, keepdims=True), jnp.sum(wide[FR:], axis=0, keepdims=True)], axis=0
    )


def affine(message, gain, bias, per, to_channels):
    entries = float(HEIGHT * COLS * per)
    mean = message[0:1] / entries
    inv = lax.rsqrt(message[1:2] / entries - mean * mean + EPS)
    stacked = jnp.concatenate([jnp.broadcast_to(mean, (FR, 128)), jnp.broadcast_to(inv, (FR, 128))], axis=0)
    wide = exact_dot(jnp.where(frame_lanes(2 * FR), stacked, 0.0), to_channels)
    scale = wide[FR:] * gain
    return scale, bias - wide[:FR] * scale


def silu(v):
    half = 0.5 * v
    return half + half * jnp.tanh(half)


def shifted(a):
    zero = jnp.zeros(a.shape[:1] + (1,) + a.shape[2:], a.dtype)
    left = jnp.concatenate([zero, a[:, : COLS - 1]], axis=1)
    right = jnp.concatenate([a[:, 1:], zero], axis=1)
    return left, a, right


def kernel(
    lat, g1, b1, fk, g2, b2, sk, skw, rk, clips, out,
    xraw, fk_in, fk_pair, w1, w2, wskip, rkv, x1, hown, hraw, x2, x3, wres, acc_ref, out_v, acc2,
    mine, st_in, st_total, st_prev, mine2, st_in2, st_total2, st_prev2,
    lanes1, chans1, lanes2, chans2,
    load_sem, halo_s, halo_r, stat_s, stat_r, pair_s, pair_r,
    zs, zr, xs, xr, ps, pr,
):
    tm = lax.axis_index("tm")
    tile = lax.axis_index("tile")
    y, x = tm // NX, lax.rem(tm, NX)
    z, core = tile // 2, lax.rem(tile, 2)
    step = 1 - 2 * core
    tm_next, tm_prev = lax.rem(tm + 1, SPANS), lax.rem(tm + SPANS - 1, SPANS)
    up, down = lax.rem(tile + TILES - 1, TILES), lax.rem(tile + 1, TILES)
    partner = (tm, tile + step)

    def along_x(by):
        return (y * NX + lax.rem(x + by + 2 * NX, NX), tile)

    def along_z(by):
        return (tm, lax.rem(z + by + 2 * NZ, NZ) * 2 + core)

    def remote(src, dst, send, recv, to):
        return pltpu.make_async_remote_copy(
            src_ref=src, dst_ref=dst, send_sem=send, recv_sem=recv,
            device_id=to, device_id_type=pl.DeviceIdType.MESH,
        )

    loads = [
        pltpu.make_async_copy(lat, xraw.at[2:6, 1:5], load_sem.at[0]),
        pltpu.make_async_copy(fk, fk_in, load_sem.at[1]),
        pltpu.make_async_copy(sk, w2, load_sem.at[2]),
        pltpu.make_async_copy(skw, wskip, load_sem.at[3]),
        pltpu.make_async_copy(rk, rkv, load_sem.at[4]),
    ]
    for load in loads:
        load.start()

    barrier = pltpu.get_barrier_semaphore()
    near = [along_x(1), along_x(-1), (tm_prev, tile), (tm_prev, up), (tm_prev, down)]

    def greet(to):
        pl.semaphore_signal(barrier, inc=1, device_id=to, device_id_type=pl.DeviceIdType.MESH)

    def greet_group(i, carry):
        greet((tm, lax.rem(tile + i, TILES)))
        return carry

    lax.fori_loop(1, TILES, greet_group, 0)
    for to in near:
        greet(to)

    lanes1[...] = member(CIN // GROUPS, False)
    chans1[...] = member(CIN // GROUPS, True)
    lanes2[...] = member(CMID // GROUPS, False)
    chans2[...] = member(CMID // GROUPS, True)

    loads[0].wait()
    sums, squares = [], []
    for f in range(FR):
        v = xraw[2 + f, 1:5].astype(F32).reshape(ROWS * COLS, CIN)
        sums.append(jnp.sum(v, axis=0, keepdims=True))
        squares.append(jnp.sum(v * v, axis=0, keepdims=True))
    mine[...] = partial_stats(jnp.concatenate(sums), jnp.concatenate(squares), lanes1[...])
    loads[4].wait()
    for a in range(2):
        for tap in range(2):
            if a == 0:
                q = [rkv[0, d].astype(F32) for d in range(3)] if tap == 0 else [
                    rkv[1, d].astype(F32) + rkv[2, d].astype(F32) for d in range(3)
                ]
            else:
                q = [rkv[0, d].astype(F32) + rkv[1, d].astype(F32) for d in range(3)] if tap == 0 else [
                    rkv[2, d].astype(F32) for d in range(3)
                ]
            none = jnp.zeros_like(q[0])
            cols = [
                jnp.concatenate([q[0], none], axis=1),
                jnp.concatenate([q[1] + q[2], q[0] + q[1]], axis=1),
                jnp.concatenate([none, q[2]], axis=1),
            ]
            for d in range(3):
                wres[a, (tap * 3 + d) * CMID : (tap * 3 + d + 1) * CMID, :] = cols[d].astype(BF16)

    loads[1].wait()
    pl.semaphore_wait(barrier, TILES - 1 + len(near))

    def exchange(src, at_in, phase):
        for far in range(8, 0, -1):
            for i in (far, TILES - far)[: 2 if far < 8 else 1]:
                remote(
                    src, at_in.at[i - 1], stat_s.at[phase, 0], stat_r.at[phase, 0],
                    (tm, lax.rem(tile + i, TILES)),
                ).start()

    def exchange_copy(at_in, phase):
        return remote(at_in, at_in, stat_s.at[phase, 0], stat_r.at[phase, 0], partner)

    def relay(total, at_prev, phase):
        return remote(total, at_prev, stat_s.at[phase, 1], stat_r.at[phase, 1], (tm_next, tile))

    def halo_copies(ref, rim, phase):
        lo, hi = rim, rim + ROWS
        head, tail = (lo, lo + rim), (hi - rim, hi)
        cuts = [
            ((2, 6), head, (2, 6), (hi, hi + rim), (tm, up)),
            ((2, 6), tail, (2, 6), (0, rim), (tm, down)),
            ((4, 6), (lo, hi), (0, 2), (lo, hi), (tm_next, tile)),
            ((4, 6), head, (0, 2), (hi, hi + rim), (tm_next, up)),
            ((4, 6), tail, (0, 2), (0, rim), (tm_next, down)),
        ]
        return [
            remote(
                ref.at[a[0] : a[1], b[0] : b[1]], ref.at[c[0] : c[1], d[0] : d[1]],
                halo_s.at[phase, i], halo_r.at[phase, i], to,
            )
            for i, (a, b, c, d, to) in enumerate(cuts)
        ]

    pair = remote(fk_in, fk_pair, pair_s.at[0], pair_r.at[0], partner)
    pair.start()
    exchange(mine, st_in, 0)

    pair.wait_recv()

    def both_halves(t):
        a, b = fk_in[t].astype(F32), fk_pair[t].astype(F32)
        return jnp.concatenate([jnp.where(core == 1, b, a), jnp.where(core == 1, a, b)], axis=0)

    for p in range(14):
        even = both_halves(2 * p)
        w1[3 * p, z] = even[:, :128].astype(BF16)
        if p < 13:
            odd = both_halves(2 * p + 1)
            w1[3 * p + 1, z] = odd[:, :128].astype(BF16)
            rest = jnp.concatenate([even[:, 128:], odd[:, 128:]], axis=1)
            w1[3 * p + 2, z] = rest.astype(BF16)
        else:
            rest = jnp.concatenate([even[:, 128:], jnp.zeros_like(even[:, 128:])], axis=1)
            w1[3 * p + 1, z] = rest.astype(BF16)

    my_x = XU * x
    blocks = 4

    def chip_of(k):
        return lax.rem(z - step * (k + 1) + 2 * NZ, NZ)

    def region(unit, count, chip, half):
        first = (count + 1) // 2
        if half is not None:
            unit, count = (unit, first) if half == 0 else (unit + first, count - first)
        return w1.at[pl.ds(unit, count), chip]

    def halves(k, body):
        if k < blocks - 1:
            body(None)
        else:
            for half in (0, 1):
                pl.when(core == half)(functools.partial(body, half))

    def z_copy(k, c, half):
        if c == 0:
            source, by = (z, k + 1) if k < 2 else (chip_of(1), k - 1)
            ref = region(my_x, XU, source, half)
        else:
            ref, by = region(XT, ZT, chip_of(k - 1), half), 1
        return remote(ref, ref, zs.at[k, c], zr.at[k, c], along_z(step * by))

    def x_copy(k, hop, half):
        unit = my_x if hop != 1 else XU * lax.rem(x - step + NX, NX)
        ref = region(unit, XU, chip_of(k), half)
        return remote(ref, ref, xs.at[k, hop], xr.at[k, hop], along_x((step, step, -step)[hop]))

    def p_copy(k, i, half):
        by = (-step, -2 * step, step, 0, None)[i]
        if by is None:
            ref = region(XT, ZT, chip_of(k), half)
        else:
            ref = region(XU * lax.rem(x + by + NX, NX), XU, chip_of(k), half)
        return remote(ref, ref, ps.at[k, i], pr.at[k, i], partner)

    def z_start():
        for k in (1, 0):
            z_copy(k, 0, None).start()
        z_copy(0, 1, None).start()

    def zx_arrived(k):
        def body(half):
            z_copy(k, 0, half).wait_recv()
            x_copy(k, 0, half).start()
            x_copy(k, 2, half).start()
            p_copy(k, 3, half).start()

        if k == 1:
            z_copy(1, 0, None).wait_recv()
            halves(3, lambda half: z_copy(3, 0, half).start())
            z_copy(2, 0, None).start()
            x_copy(1, 0, None).start()
            x_copy(1, 2, None).start()
            p_copy(1, 3, None).start()
        else:
            halves(k, body)

    def zz_arrived(k):
        halves(k, lambda half: z_copy(k, 1, half).wait_recv())
        if k + 1 < blocks:
            halves(k + 1, lambda half: z_copy(k + 1, 1, half).start())
        halves(k, lambda half: p_copy(k, 4, half).start())

    def x_arrived(k, hop):
        def body(half):
            x_copy(k, hop, half).wait_recv()
            if hop == 0:
                x_copy(k, 1, half).start()
            p_copy(k, hop, half).start()

        halves(k, body)

    z_start()
    halos = halo_copies(xraw, 1, 0)
    for copy in halos:
        copy.start()

    starts_here = span_start(clips, tm)
    keep_prev = jnp.where(starts_here, 0.0, 1.0).astype(F32)
    keep_top = jnp.where(tile == 0, 0.0, 1.0).astype(F32)
    keep_bottom = jnp.where(tile == TILES - 1, 0.0, 1.0).astype(F32)

    def first_act(f, scale, shift):
        a = silu(xraw[f].astype(F32) * scale[None, None, :] + shift[None, None, :])
        if f < 2:
            a = a * keep_prev
        a = jnp.concatenate([a[0:1] * keep_top, a[1:5], a[5:6] * keep_bottom], axis=0)
        for d, part in enumerate(shifted(a)):
            x1[f, :, :, d * CIN : (d + 1) * CIN] = part.astype(BF16)

    zx_arrived(1)
    exchange_copy(st_in, 0).wait_recv()
    st_total[...] = jnp.sum(st_in[...], axis=0) + mine[...]
    relayed = relay(st_total, st_prev, 0)
    relayed.start()
    zx_arrived(0)
    zz_arrived(0)
    x_arrived(1, 0)
    x_arrived(1, 2)
    zx_arrived(3)
    zx_arrived(2)
    x_arrived(0, 0)
    x_arrived(0, 2)
    zz_arrived(1)
    for copy in halos[:2]:
        copy.wait_recv()
    gain, bias = g1[...].reshape(1, CIN), b1[...].reshape(1, CIN)
    scale, shift = affine(st_total[...], gain, bias, CIN // GROUPS, chans1[...])
    first_act(2, scale[0], shift[0])
    first_act(3, scale[1], shift[1])
    x_arrived(3, 0)
    x_arrived(3, 2)
    first_act(4, scale[2], shift[2])
    first_act(5, scale[3], shift[3])
    x_arrived(1, 1)
    x_arrived(2, 2)
    x_arrived(2, 0)
    relayed.wait_recv()
    for copy in halos[2:]:
        copy.wait_recv()
    scale, shift = affine(st_prev[...], gain, bias, CIN // GROUPS, chans1[...])
    first_act(0, scale[2], shift[2])
    first_act(1, scale[3], shift[3])
    zz_arrived(2)
    x_arrived(0, 1)
    x_arrived(3, 1)
    zz_arrived(3)
    x_arrived(2, 1)

    for k in range(blocks):
        for i in range(5):
            halves(k, lambda half: p_copy(k, i, None if half is None else 1 - half).wait_recv())

    def tap_window(t):
        s, rest = divmod(t, 9)
        dy, dx = divmod(rest, 3)
        window = x1[s : s + FR, dy : dy + ROWS, :, dx * CIN : (dx + 1) * CIN]
        return window.reshape(FR * ROWS * COLS, CIN)

    def conv1(pairs, first):
        total = [None, None] if first else [acc_ref[0], acc_ref[1]]
        for p in pairs:
            rest = w1[3 * p + (2 if p < 13 else 1)].reshape(CIN, 128)
            for odd in range(2 if p < 13 else 1):
                weights = jnp.concatenate([w1[3 * p + odd].reshape(CIN, 128), rest], axis=1)
                term = jnp.dot(tap_window(2 * p + odd), weights, preferred_element_type=F32)
                total[odd] = term if total[odd] is None else total[odd] + term
        acc_ref[0], acc_ref[1] = total

    conv1(range(14), True)

    even, odd = acc_ref[0], acc_ref[1]
    hidden = jnp.concatenate([even[:, :128] + odd[:, :128], even[:, 128:192] + odd[:, 192:]], axis=1)
    hidden = hidden.reshape(FR, ROWS * COLS, CMID)
    hown[...] = hidden.reshape(FR, ROWS, COLS, CMID)
    hraw[2:6, 2:6] = hidden.reshape(FR, ROWS, COLS, CMID).astype(BF16)
    halos2 = halo_copies(hraw, 2, 1)
    for copy in halos2:
        copy.start()
    mine2[...] = partial_stats(jnp.sum(hidden, axis=1), jnp.sum(hidden * hidden, axis=1), lanes2[...])
    exchange(mine2, st_in2, 1)

    loads[3].wait()
    loads[2].wait()
    shortcut = lax.dot_general(
        xraw[2:6].reshape(FR * 6 * COLS, CIN), wskip[...], (((1,), (1,)), ((), ())),
        preferred_element_type=F32,
    )

    exchange_copy(st_in2, 1).wait_recv()
    st_total2[...] = jnp.sum(st_in2[...], axis=0) + mine2[...]
    relayed2 = relay(st_total2, st_prev2, 1)
    relayed2.start()
    for copy in halos2[:2]:
        copy.wait_recv()

    def second_act(f, scale, shift):
        if f >= 2:
            v = jnp.concatenate(
                [hraw[f, 0:2].astype(F32), hown[f - 2], hraw[f, 6:8].astype(F32)], axis=0
            )
        else:
            v = hraw[f].astype(F32)
        a = silu(v * scale[None, None, :] + shift[None, None, :])
        if f < 2:
            a = a * keep_prev
        a = jnp.concatenate([a[0:2] * keep_top, a[2:6], a[6:8] * keep_bottom], axis=0)
        x2[f] = jnp.concatenate(shifted(a), axis=-1).astype(BF16)

    def conv2(s):
        total = None
        for dy in range(3):
            window = x2[s : s + FR, dy : dy + 6].reshape(FR * 6 * COLS, 3 * CMID)
            weights = w2[9 * s + 3 * dy : 9 * s + 3 * dy + 3].reshape(3 * CMID, CMID)
            term = jnp.dot(window, weights, preferred_element_type=F32)
            total = term if total is None else total + term
        return total

    gain, bias = g2[...].reshape(1, CMID), b2[...].reshape(1, CMID)
    scale, shift = affine(st_total2[...], gain, bias, CMID // GROUPS, chans2[...])
    for f in range(FR):
        second_act(2 + f, scale[f], shift[f])
    acc2[...] = shortcut + conv2(2)
    relayed2.wait_recv()
    for copy in halos2[2:]:
        copy.wait_recv()
    scale, shift = affine(st_prev2[...], gain, bias, CMID // GROUPS, chans2[...])
    second_act(0, scale[2], shift[2])
    second_act(1, scale[3], shift[3])

    total = acc2[...] + conv2(1) + conv2(0)
    block = total.astype(BF16).astype(F32).reshape(FR, 6, COLS, CMID)
    for f in range(FR):
        a = jnp.concatenate(
            [block[f, 0:1] * keep_top, block[f, 1:5], block[f, 5:6] * keep_bottom], axis=0
        )
        x3[f] = jnp.concatenate(shifted(a), axis=-1).astype(BF16)

    for a in range(2):
        window = jnp.concatenate(
            [x3[:, a : a + ROWS], x3[:, a + 1 : a + 1 + ROWS]], axis=-1
        ).reshape(FR * ROWS * COLS, 6 * CMID)
        res = jnp.dot(window, wres[a], preferred_element_type=F32)
        res = res.astype(BF16).reshape(FR, ROWS, COLS, 2 * COUT)
        out_v[:, :, a] = res
    store = pltpu.make_async_copy(out_v, out, load_sem.at[5])
    store.start()

    pair.wait_send()
    for copy in halos + halos2:
        copy.wait_send()
    for copy in (exchange_copy(st_in, 0), exchange_copy(st_in2, 1), relayed, relayed2):
        copy.wait_send()

    def drain(k, half):
        for c in range(2):
            z_copy(k, c, half).wait_send()
        for hop in range(3):
            x_copy(k, hop, half).wait_send()
        for i in range(5):
            p_copy(k, i, half).wait_send()

    for k in range(blocks):
        halves(k, functools.partial(drain, k))
    store.wait()


def span_start(clips, tm):
    start, hit = jnp.int32(0), tm == 0
    for j in range(3):
        start = start + clips[j]
        hit = hit | (start == tm)
    return hit


def shards(
    latents, first_gain, first_bias, first_kernel, second_gain, second_bias,
    second_kernel, skip_weight, resample_kernel, clip_spans,
):
    fk = jnp.transpose(first_kernel, (1, 2, 3, 0, 4)).reshape(27, SHARD, CMID)
    sk = jnp.transpose(second_kernel, (1, 2, 3, 0, 4)).reshape(27, CMID, CMID)
    anywhere = pl.BlockSpec(memory_space=pl.ANY)
    vmem = pl.BlockSpec(memory_space=pltpu.VMEM)
    smem = pl.BlockSpec(memory_space=pltpu.SMEM)
    dma = pltpu.SemaphoreType.DMA
    out = pl.pallas_call(
        kernel,
        out_shape=jax.ShapeDtypeStruct((FR, ROWS, 2, COLS, 2 * COUT), BF16),
        in_specs=[anywhere, vmem, vmem, anywhere, vmem, vmem, anywhere, anywhere, anywhere, smem],
        out_specs=anywhere,
        scratch_shapes=[
            pltpu.VMEM((6, 6, COLS, CIN), BF16),
            pltpu.VMEM((27, SHARD, CMID), BF16),
            pltpu.VMEM((27, SHARD, CMID), BF16),
            pltpu.VMEM((UNITS, NZ, UNIT, 128), BF16),
            pltpu.VMEM((27, CMID, CMID), BF16),
            pltpu.VMEM((CMID, CIN), BF16),
            pltpu.VMEM((3, 3, CMID, COUT), BF16),
            pltpu.VMEM((6, 6, COLS, 3 * CIN), BF16),
            pltpu.VMEM((FR, ROWS, COLS, CMID), F32),
            pltpu.VMEM((6, 8, COLS, CMID), BF16),
            pltpu.VMEM((6, 8, COLS, 3 * CMID), BF16),
            pltpu.VMEM((FR, 6, COLS, 3 * CMID), BF16),
            pltpu.VMEM((2, 6 * CMID, 2 * COUT), BF16),
            pltpu.VMEM((2, FR * ROWS * COLS, 256), F32),
            pltpu.VMEM((FR, ROWS, 2, COLS, 2 * COUT), BF16),
            pltpu.VMEM((FR * 6 * COLS, CMID), F32),
            pltpu.VMEM((2, 128), F32),
            pltpu.VMEM((TILES - 1, 2, 128), F32),
            pltpu.VMEM((2, 128), F32),
            pltpu.VMEM((2, 128), F32),
            pltpu.VMEM((2, 128), F32),
            pltpu.VMEM((TILES - 1, 2, 128), F32),
            pltpu.VMEM((2, 128), F32),
            pltpu.VMEM((2, 128), F32),
            pltpu.VMEM((CIN, 128), BF16),
            pltpu.VMEM((128, CIN), BF16),
            pltpu.VMEM((CMID, 128), BF16),
            pltpu.VMEM((128, CMID), BF16),
            dma((6,)),
            dma((2, 5)), dma((2, 5)),
            dma((2, 2)), dma((2, 2)),
            dma((1,)), dma((1,)),
            dma((4, 2)), dma((4, 2)),
            dma((4, 3)), dma((4, 3)),
            dma((4, 5)), dma((4, 5)),
        ],
        compiler_params=pltpu.CompilerParams(
            collective_id=0, has_side_effects=True, vmem_limit_bytes=56 * 2**20
        ),
    )(
        latents, first_gain, first_bias, fk,
        second_gain, second_bias, sk, skip_weight.T,
        resample_kernel, clip_spans,
    )
    return out.reshape(FR, 2 * ROWS, COLS, 2 * COUT)


def solution(mesh):
    in_specs = (
        P("tm", "tile", None, None), P(), P(), P("tile", None, None, None, None),
        P(), P(), P(), P(), P(), P(),
    )
    return jax.shard_map(
        shards, mesh=mesh, in_specs=in_specs, out_specs=P("tm", "tile", None, None), check_vma=False
    )
```

time: 57.3 us -> 55.4 us (0.967); the launches traced: 56.3 us -> 55.2 us
  Pallas kernels: 54.6 us -> 53.5 us
    pallas_call x1, Pallas kernels: 54.6 us -> 53.5 us  [shards(): pl.pallas_call(kernel, out_shape=jax.ShapeDtypeStruct((FR, ROWS, 2, COLS,...]
where the time goes in v3:
time: 55.4 us; the launch traced here: 55.2 us
  Pallas kernels  53.5 us (97%)
  local copies, waits for them, and re-layouts  1.67 us (3%)
    pallas_call x1, Pallas kernels, shards(): pl.pallas_call(kernel, out_shape=jax.ShapeDtypeStruct((FR, ROWS, 2, COLS,...  53.5 us
    unnamed x1, local copies, waits for them, and re-layouts  1.67 us

profile of v3, /device:TPU:1, one launch (start us, length us, event | category | flops | bytes accessed | tf_op | source)
XLA Modules:
  0.0 55.2 jit_solution(14802741903138419749)
XLA Ops:
  0.0 53.5 %shard_map.100 = bf16[4,4,2,16,192]{4,3,2,1,0:T(8,128)(2,1)} custom-call(bf16[4,4,16,384]{3,2,1,0:T(8,128)(2,1)} %lat.1, f32[384]{0:T(512)} %g1.1, f32[384]{0:T(512)} %b1.1, bf16[27,24,192]{2,1,0:T(8,128)(2,1)} %bitcast.10, f32[192]{0:T(256)} %g2.1, f32[192]{0:T(256)} %b2.1, bf16[27,192,192]{2,1,0:T(8,128)(2,1)} %bitcast.8, bf16[192,384]{1,0:T(8,128)(2,1)} %bitcast.11, ...), custom_call_target="tpu_custom_call" | custom-call | tf_op jit(solution)/shard_map/pallas_call | solution.py:496
  53.5 1.7 %copy.12 = bf16[4,8,16,192]{3,2,1,0:T(8,128)(2,1)} copy(bf16[4,8,16,192]{3,2,1,0:T(8,128)(2,1)} %bitcast.9) | data formatting | bytes 393216

commit v4 on v3

--- a/solution.py
+++ b/solution.py
@@ -19,9 +19,10 @@
 SHARD = CIN // TILES
 UNIT = 2 * SHARD
 UNITS = 41
-XU = 8
-XT = XU * NX
-ZT = UNITS - XT
+XU, YU = 4, 2
+XT, YT = XU * NX, YU * NY
+ZT = UNITS - XT - YT
+PAD = 256
 HEIGHT = ROWS * TILES
 
 
@@ -83,11 +84,11 @@
 
 def kernel(
     lat, g1, b1, fk, g2, b2, sk, skw, rk, clips, out,
-    xraw, fk_in, fk_pair, w1, w2, wskip, rkv, x1, hown, hraw, x2, x3, wres, acc_ref, out_v, acc2,
+    xraw, fk_in, fk_pair, w1, wy, w2, wskip, rkv, x1, hown, hraw, x2, x3, wres, acc_ref, out_v, acc2,
     mine, st_in, st_total, st_prev, mine2, st_in2, st_total2, st_prev2,
     lanes1, chans1, lanes2, chans2,
     load_sem, halo_s, halo_r, stat_s, stat_r, pair_s, pair_r,
-    zs, zr, xs, xr, ps, pr,
+    zs, zr, xs, xr, ys, yr, ps, pr,
 ):
     tm = lax.axis_index("tm")
     tile = lax.axis_index("tile")
@@ -101,6 +102,9 @@
     def along_x(by):
         return (y * NX + lax.rem(x + by + 2 * NX, NX), tile)
 
+    def along_y(by):
+        return (lax.rem(y + by + 2 * NY, NY) * NX + x, tile)
+
     def along_z(by):
         return (tm, lax.rem(z + by + 2 * NZ, NZ) * 2 + core)
 
@@ -121,7 +125,8 @@
         load.start()
 
     barrier = pltpu.get_barrier_semaphore()
-    near = [along_x(1), along_x(-1), (tm_prev, tile), (tm_prev, up), (tm_prev, down)]
+    near = [along_x(1), along_x(-1), along_y(1), along_y(-1), along_y(2), along_y(-2)]
+    near += [(tm_prev, tile), (tm_prev, up), (tm_prev, down)]
 
     def greet(to):
         pl.semaphore_signal(barrier, inc=1, device_id=to, device_id_type=pl.DeviceIdType.MESH)
@@ -207,21 +212,26 @@
 
     pair.wait_recv()
 
+    def unit_ref(u):
+        if XT <= u < XT + YT:
+            return wy.at[(u - XT) // YU, (u - XT) % YU]
+        return w1.at[u]
+
     def both_halves(t):
         a, b = fk_in[t].astype(F32), fk_pair[t].astype(F32)
         return jnp.concatenate([jnp.where(core == 1, b, a), jnp.where(core == 1, a, b)], axis=0)
 
     for p in range(14):
         even = both_halves(2 * p)
-        w1[3 * p, z] = even[:, :128].astype(BF16)
+        unit_ref(3 * p)[z] = even[:, :128].astype(BF16)
         if p < 13:
             odd = both_halves(2 * p + 1)
-            w1[3 * p + 1, z] = odd[:, :128].astype(BF16)
+            unit_ref(3 * p + 1)[z] = odd[:, :128].astype(BF16)
             rest = jnp.concatenate([even[:, 128:], odd[:, 128:]], axis=1)
-            w1[3 * p + 2, z] = rest.astype(BF16)
+            unit_ref(3 * p + 2)[z] = rest.astype(BF16)
         else:
             rest = jnp.concatenate([even[:, 128:], jnp.zeros_like(even[:, 128:])], axis=1)
-            w1[3 * p + 1, z] = rest.astype(BF16)
+            unit_ref(3 * p + 1)[z] = rest.astype(BF16)
 
     my_x = XU * x
     blocks = 4
@@ -234,6 +244,9 @@
         if half is not None:
             unit, count = (unit, first) if half == 0 else (unit + first, count - first)
         return w1.at[pl.ds(unit, count), chip]
+
+    def y_region(at, chip, half):
+        return wy.at[at, :, chip] if half is None else wy.at[at, half, chip]
 
     def halves(k, body):
         if k < blocks - 1:
@@ -243,11 +256,12 @@
                 pl.when(core == half)(functools.partial(body, half))
 
     def z_copy(k, c, half):
-        if c == 0:
-            source, by = (z, k + 1) if k < 2 else (chip_of(1), k - 1)
-            ref = region(my_x, XU, source, half)
+        if c < 2:
+            ref = region(my_x, XU, z, half) if c == 0 else y_region(y, z, half)
+            by = k + 1
         else:
-            ref, by = region(XT, ZT, chip_of(k - 1), half), 1
+            ref = region(XT + YT, ZT, z if k < 2 else chip_of(1), half)
+            by = k + 1 if k < 2 else k - 1
         return remote(ref, ref, zs.at[k, c], zr.at[k, c], along_z(step * by))
 
     def x_copy(k, hop, half):
@@ -255,18 +269,36 @@
         ref = region(unit, XU, chip_of(k), half)
         return remote(ref, ref, xs.at[k, hop], xr.at[k, hop], along_x((step, step, -step)[hop]))
 
+    def y_copy(k, hop, half):
+        origin = {2: -2 * step, 3: -2 * step, 6: 2 * step}.get(hop, 0)
+        by = (step, 2 * step, step, 2 * step, -step, -2 * step, -step)[hop]
+        ref = y_region(lax.rem(y + origin + NY, NY), chip_of(k), half)
+        return remote(ref, ref, ys.at[k, hop], yr.at[k, hop], along_y(by))
+
     def p_copy(k, i, half):
-        by = (-step, -2 * step, step, 0, None)[i]
-        if by is None:
-            ref = region(XT, ZT, chip_of(k), half)
+        if i < 4:
+            by = (-step, -2 * step, step, 0)[i]
+            ref = region(XU * lax.rem(x + by + NX, NX), XU, chip_of(k), half)
+        elif i == 5:
+            ref = region(XT + YT, ZT, chip_of(k), half)
         else:
-            ref = region(XU * lax.rem(x + by + NX, NX), XU, chip_of(k), half)
+            ref = y_region(slice(None), chip_of(k), half)
         return remote(ref, ref, ps.at[k, i], pr.at[k, i], partner)
 
     def z_start():
+        for c in (1, 0):
+            for k in range(blocks):
+                halves(k, lambda half: z_copy(k, c, half).start())
         for k in (1, 0):
-            z_copy(k, 0, None).start()
-        z_copy(0, 1, None).start()
+            z_copy(k, 2, None).start()
+
+    def zy_arrived(k):
+        def body(half):
+            z_copy(k, 1, half).wait_recv()
+            for hop in (1, 5, 0, 4):
+                y_copy(k, hop, half).start()
+
+        halves(k, body)
 
     def zx_arrived(k):
         def body(half):
@@ -275,21 +307,34 @@
             x_copy(k, 2, half).start()
             p_copy(k, 3, half).start()
 
+        halves(k, body)
+
+    def zz_arrived(k):
+        halves(k, lambda half: z_copy(k, 2, half).wait_recv())
         if k == 1:
-            z_copy(1, 0, None).wait_recv()
-            halves(3, lambda half: z_copy(3, 0, half).start())
-            z_copy(2, 0, None).start()
-            x_copy(1, 0, None).start()
-            x_copy(1, 2, None).start()
-            p_copy(1, 3, None).start()
-        else:
-            halves(k, body)
-
-    def zz_arrived(k):
-        halves(k, lambda half: z_copy(k, 1, half).wait_recv())
-        if k + 1 < blocks:
-            halves(k + 1, lambda half: z_copy(k + 1, 1, half).start())
-        halves(k, lambda half: p_copy(k, 4, half).start())
+            halves(3, lambda half: z_copy(3, 2, half).start())
+            z_copy(2, 2, None).start()
+        halves(k, lambda half: p_copy(k, 5, half).start())
+
+    def y_arrived(k):
+        def body(half):
+            for hop in (0, 4):
+                y_copy(k, hop, half).wait_recv()
+            y_copy(k, 1, half).wait_recv()
+            y_copy(k, 3, half).start()
+            y_copy(k, 2, half).start()
+            y_copy(k, 5, half).wait_recv()
+            y_copy(k, 6, half).start()
+
+        halves(k, body)
+
+    def y_last(k):
+        def body(half):
+            for hop in (6, 2, 3):
+                y_copy(k, hop, half).wait_recv()
+            p_copy(k, 4, half).start()
+
+        halves(k, body)
 
     def x_arrived(k, hop):
         def body(half):
@@ -318,48 +363,61 @@
         for d, part in enumerate(shifted(a)):
             x1[f, :, :, d * CIN : (d + 1) * CIN] = part.astype(BF16)
 
-    zx_arrived(1)
+    zy_arrived(0)
+    zy_arrived(1)
+    zy_arrived(2)
     exchange_copy(st_in, 0).wait_recv()
     st_total[...] = jnp.sum(st_in[...], axis=0) + mine[...]
     relayed = relay(st_total, st_prev, 0)
     relayed.start()
     zx_arrived(0)
-    zz_arrived(0)
+    zy_arrived(3)
+    zx_arrived(1)
+    y_arrived(0)
+    zx_arrived(2)
+    y_arrived(1)
+    x_arrived(0, 0)
+    x_arrived(0, 2)
+    y_arrived(2)
+    zx_arrived(3)
     x_arrived(1, 0)
     x_arrived(1, 2)
-    zx_arrived(3)
-    zx_arrived(2)
-    x_arrived(0, 0)
-    x_arrived(0, 2)
     zz_arrived(1)
+    y_arrived(3)
     for copy in halos[:2]:
         copy.wait_recv()
     gain, bias = g1[...].reshape(1, CIN), b1[...].reshape(1, CIN)
     scale, shift = affine(st_total[...], gain, bias, CIN // GROUPS, chans1[...])
     first_act(2, scale[0], shift[0])
     first_act(3, scale[1], shift[1])
+    x_arrived(2, 0)
+    x_arrived(2, 2)
+    y_last(0)
+    zz_arrived(0)
+    first_act(4, scale[2], shift[2])
+    first_act(5, scale[3], shift[3])
+    x_arrived(0, 1)
+    y_last(1)
     x_arrived(3, 0)
     x_arrived(3, 2)
-    first_act(4, scale[2], shift[2])
-    first_act(5, scale[3], shift[3])
-    x_arrived(1, 1)
-    x_arrived(2, 2)
-    x_arrived(2, 0)
     relayed.wait_recv()
     for copy in halos[2:]:
         copy.wait_recv()
     scale, shift = affine(st_prev[...], gain, bias, CIN // GROUPS, chans1[...])
     first_act(0, scale[2], shift[2])
+    y_last(2)
+    x_arrived(1, 1)
     first_act(1, scale[3], shift[3])
-    zz_arrived(2)
-    x_arrived(0, 1)
-    x_arrived(3, 1)
+    y_last(3)
     zz_arrived(3)
     x_arrived(2, 1)
-
-    for k in range(blocks):
-        for i in range(5):
-            halves(k, lambda half: p_copy(k, i, None if half is None else 1 - half).wait_recv())
+    zz_arrived(2)
+    x_arrived(3, 1)
+
+    def partner_wait(parts):
+        for k in range(blocks):
+            for i in parts:
+                halves(k, lambda half: p_copy(k, i, None if half is None else 1 - half).wait_recv())
 
     def tap_window(t):
         s, rest = divmod(t, 9)
@@ -370,14 +428,17 @@
     def conv1(pairs, first):
         total = [None, None] if first else [acc_ref[0], acc_ref[1]]
         for p in pairs:
-            rest = w1[3 * p + (2 if p < 13 else 1)].reshape(CIN, 128)
+            rest = unit_ref(3 * p + (2 if p < 13 else 1))[...].reshape(CIN, 128)
             for odd in range(2 if p < 13 else 1):
-                weights = jnp.concatenate([w1[3 * p + odd].reshape(CIN, 128), rest], axis=1)
+                weights = jnp.concatenate([unit_ref(3 * p + odd)[...].reshape(CIN, 128), rest], axis=1)
                 term = jnp.dot(tap_window(2 * p + odd), weights, preferred_element_type=F32)
                 total[odd] = term if total[odd] is None else total[odd] + term
         acc_ref[0], acc_ref[1] = total
 
-    conv1(range(14), True)
+    partner_wait((4, 5))
+    conv1(range(6, 14), True)
+    partner_wait((0, 1, 2, 3))
+    conv1(range(0, 6), False)
 
     even, odd = acc_ref[0], acc_ref[1]
     hidden = jnp.concatenate([even[:, :128] + odd[:, :128], even[:, 128:192] + odd[:, 192:]], axis=1)
@@ -463,11 +524,13 @@
         copy.wait_send()
 
     def drain(k, half):
-        for c in range(2):
+        for c in range(3):
             z_copy(k, c, half).wait_send()
         for hop in range(3):
             x_copy(k, hop, half).wait_send()
-        for i in range(5):
+        for hop in range(7):
+            y_copy(k, hop, half).wait_send()
+        for i in range(6):
             p_copy(k, i, half).wait_send()
 
     for k in range(blocks):
@@ -503,6 +566,7 @@
             pltpu.VMEM((27, SHARD, CMID), BF16),
             pltpu.VMEM((27, SHARD, CMID), BF16),
             pltpu.VMEM((UNITS, NZ, UNIT, 128), BF16),
+            pltpu.VMEM((NY, YU, NZ, UNIT, 128), BF16),
             pltpu.VMEM((27, CMID, CMID), BF16),
             pltpu.VMEM((CMID, CIN), BF16),
             pltpu.VMEM((3, 3, CMID, COUT), BF16),
@@ -531,9 +595,10 @@
             dma((2, 5)), dma((2, 5)),
             dma((2, 2)), dma((2, 2)),
             dma((1,)), dma((1,)),
-            dma((4, 2)), dma((4, 2)),
             dma((4, 3)), dma((4, 3)),
-            dma((4, 5)), dma((4, 5)),
+            dma((4, 3)), dma((4, 3)),
+            dma((4, 7)), dma((4, 7)),
+            dma((4, 6)), dma((4, 6)),
         ],
         compiler_params=pltpu.CompilerParams(
             collective_id=0, has_side_effects=True, vmem_limit_bytes=56 * 2**20

time: 55.4 us -> 52.8 us (0.953)
  Pallas kernels: 53.5 us -> 51 us
    pallas_call x1, Pallas kernels: 53.5 us -> 51 us  [shards(): pl.pallas_call(kernel, out_shape=jax.ShapeDtypeStruct((FR, ROWS, 2, COLS,...]
where the time goes in v4:
time: 52.8 us; the launch traced here: 52.6 us
  Pallas kernels  51 us (97%)
  local copies, waits for them, and re-layouts  1.67 us (3%)
    pallas_call x1, Pallas kernels, shards(): pl.pallas_call(kernel, out_shape=jax.ShapeDtypeStruct((FR, ROWS, 2, COLS,...  51 us
    unnamed x1, local copies, waits for them, and re-layouts  1.67 us

profile of v4, /device:TPU:1, one launch (start us, length us, event | category | flops | bytes accessed | tf_op | source)
XLA Modules:
  0.0 52.6 jit_solution(14320831527165599626)
XLA Ops:
  0.0 51.0 %shard_map.100 = bf16[4,4,2,16,192]{4,3,2,1,0:T(8,128)(2,1)} custom-call(bf16[4,4,16,384]{3,2,1,0:T(8,128)(2,1)} %lat.1, f32[384]{0:T(512)} %g1.1, f32[384]{0:T(512)} %b1.1, bf16[27,24,192]{2,1,0:T(8,128)(2,1)} %bitcast.10, f32[192]{0:T(256)} %g2.1, f32[192]{0:T(256)} %b2.1, bf16[27,192,192]{2,1,0:T(8,128)(2,1)} %bitcast.8, bf16[192,384]{1,0:T(8,128)(2,1)} %bitcast.11, ...), custom_call_target="tpu_custom_call" | custom-call | tf_op jit(solution)/shard_map/pallas_call | solution.py:559
  51.0 1.7 %copy.12 = bf16[4,8,16,192]{3,2,1,0:T(8,128)(2,1)} copy(bf16[4,8,16,192]{3,2,1,0:T(8,128)(2,1)} %bitcast.9) | data formatting | bytes 393216

commit v5 on v4

--- a/solution.py
+++ b/solution.py
@@ -117,7 +117,7 @@
     loads = [
         pltpu.make_async_copy(lat, xraw.at[2:6, 1:5], load_sem.at[0]),
         pltpu.make_async_copy(fk, fk_in, load_sem.at[1]),
-        pltpu.make_async_copy(sk, w2, load_sem.at[2]),
+        pltpu.make_async_copy(sk, w2.at[:, :CMID], load_sem.at[2]),
         pltpu.make_async_copy(skw, wskip, load_sem.at[3]),
         pltpu.make_async_copy(rk, rkv, load_sem.at[4]),
     ]
@@ -139,6 +139,11 @@
     for to in near:
         greet(to)
 
+    w2[:, CMID:] = jnp.zeros((27, PAD - CMID, CMID), BF16)
+    for d in range(3):
+        spare = slice(d * PAD + CMID, (d + 1) * PAD)
+        x2[:, :, :, spare] = jnp.zeros((6, 8, COLS, PAD - CMID), BF16)
+        x3[:, :, :, spare] = jnp.zeros((FR, 6, COLS, PAD - CMID), BF16)
     lanes1[...] = member(CIN // GROUPS, False)
     chans1[...] = member(CIN // GROUPS, True)
     lanes2[...] = member(CMID // GROUPS, False)
@@ -169,7 +174,8 @@
                 jnp.concatenate([none, q[2]], axis=1),
             ]
             for d in range(3):
-                wres[a, (tap * 3 + d) * CMID : (tap * 3 + d + 1) * CMID, :] = cols[d].astype(BF16)
+                wres[a, tap, d * PAD : d * PAD + CMID] = cols[d].astype(BF16)
+                wres[a, tap, d * PAD + CMID : (d + 1) * PAD] = jnp.zeros((PAD - CMID, 2 * COUT), BF16)
 
     loads[1].wait()
     pl.semaphore_wait(barrier, TILES - 1 + len(near))
@@ -427,11 +433,19 @@
 
     def conv1(pairs, first):
         total = [None, None] if first else [acc_ref[0], acc_ref[1]]
-        for p in pairs:
+
+        def operands(p, odd):
             rest = unit_ref(3 * p + (2 if p < 13 else 1))[...].reshape(CIN, 128)
-            for odd in range(2 if p < 13 else 1):
-                weights = jnp.concatenate([unit_ref(3 * p + odd)[...].reshape(CIN, 128), rest], axis=1)
-                term = jnp.dot(tap_window(2 * p + odd), weights, preferred_element_type=F32)
+            return tap_window(2 * p + odd), jnp.concatenate(
+                [unit_ref(3 * p + odd)[...].reshape(CIN, 128), rest], axis=1
+            )
+
+        for odd in range(2):
+            taps = [operands(p, odd) for p in pairs if 2 * p + odd < 27]
+            for at in range(0, len(taps), 2):
+                window = jnp.concatenate([t[0] for t in taps[at : at + 2]], axis=1)
+                weights = jnp.concatenate([t[1] for t in taps[at : at + 2]], axis=0)
+                term = jnp.dot(window, weights, preferred_element_type=F32)
                 total[odd] = term if total[odd] is None else total[odd] + term
         acc_ref[0], acc_ref[1] = total
 
@@ -443,17 +457,18 @@
     even, odd = acc_ref[0], acc_ref[1]
     hidden = jnp.concatenate([even[:, :128] + odd[:, :128], even[:, 128:192] + odd[:, 192:]], axis=1)
     hidden = hidden.reshape(FR, ROWS * COLS, CMID)
-    hown[...] = hidden.reshape(FR, ROWS, COLS, CMID)
-    hraw[2:6, 2:6] = hidden.reshape(FR, ROWS, COLS, CMID).astype(BF16)
+    mine2[...] = partial_stats(jnp.sum(hidden, axis=1), jnp.sum(hidden * hidden, axis=1), lanes2[...])
+    exchange(mine2, st_in2, 1)
+    hidden = hidden.reshape(FR, ROWS, COLS, CMID)
+    hown[...] = hidden
+    hraw[2:6, 2:6] = hidden.astype(BF16)
     halos2 = halo_copies(hraw, 2, 1)
     for copy in halos2:
         copy.start()
-    mine2[...] = partial_stats(jnp.sum(hidden, axis=1), jnp.sum(hidden * hidden, axis=1), lanes2[...])
-    exchange(mine2, st_in2, 1)
 
     loads[3].wait()
     loads[2].wait()
-    shortcut = lax.dot_general(
+    acc2[...] = lax.dot_general(
         xraw[2:6].reshape(FR * 6 * COLS, CIN), wskip[...], (((1,), (1,)), ((), ())),
         preferred_element_type=F32,
     )
@@ -476,46 +491,52 @@
         if f < 2:
             a = a * keep_prev
         a = jnp.concatenate([a[0:2] * keep_top, a[2:6], a[6:8] * keep_bottom], axis=0)
-        x2[f] = jnp.concatenate(shifted(a), axis=-1).astype(BF16)
-
-    def conv2(s):
-        total = None
-        for dy in range(3):
-            window = x2[s : s + FR, dy : dy + 6].reshape(FR * 6 * COLS, 3 * CMID)
-            weights = w2[9 * s + 3 * dy : 9 * s + 3 * dy + 3].reshape(3 * CMID, CMID)
-            term = jnp.dot(window, weights, preferred_element_type=F32)
-            total = term if total is None else total + term
+        for d, part in enumerate(shifted(a)):
+            x2[f, :, :, d * PAD : d * PAD + CMID] = part.astype(BF16)
+
+    def conv2(frames, taps, total):
+        for s in taps:
+            for dy in range(3):
+                window = x2[frames + s : frames + s + 2, dy : dy + 6].reshape(2 * 6 * COLS, 3 * PAD)
+                weights = w2[9 * s + 3 * dy : 9 * s + 3 * dy + 3].reshape(3 * PAD, CMID)
+                total = total + jnp.dot(window, weights, preferred_element_type=F32)
         return total
 
+    def finish(frames, total):
+        block = total.astype(BF16).astype(F32).reshape(2, 6, COLS, CMID)
+        for f in range(2):
+            a = jnp.concatenate(
+                [block[f, 0:1] * keep_top, block[f, 1:5], block[f, 5:6] * keep_bottom], axis=0
+            )
+            for d, part in enumerate(shifted(a)):
+                x3[frames + f, :, :, d * PAD : d * PAD + CMID] = part.astype(BF16)
+        for a in range(2):
+            res = None
+            for tap in range(2):
+                window = x3[frames : frames + 2, a + tap : a + tap + ROWS].reshape(2 * ROWS * COLS, 3 * PAD)
+                term = jnp.dot(window, wres[a, tap], preferred_element_type=F32)
+                res = term if res is None else res + term
+            out_v[frames : frames + 2, :, a] = res.astype(BF16).reshape(2, ROWS, COLS, 2 * COUT)
+        store = pltpu.make_async_copy(
+            out_v.at[frames : frames + 2], out.at[frames : frames + 2], load_sem.at[5 + frames // 2]
+        )
+        store.start()
+        return store
+
+    two = 2 * 6 * COLS
     gain, bias = g2[...].reshape(1, CMID), b2[...].reshape(1, CMID)
     scale, shift = affine(st_total2[...], gain, bias, CMID // GROUPS, chans2[...])
     for f in range(FR):
         second_act(2 + f, scale[f], shift[f])
-    acc2[...] = shortcut + conv2(2)
+    stores = [finish(2, conv2(2, (0, 1, 2), acc2[two:]))]
+    acc2[:two] = conv2(0, (2,), acc2[:two])
     relayed2.wait_recv()
     for copy in halos2[2:]:
         copy.wait_recv()
     scale, shift = affine(st_prev2[...], gain, bias, CMID // GROUPS, chans2[...])
     second_act(0, scale[2], shift[2])
     second_act(1, scale[3], shift[3])
-
-    total = acc2[...] + conv2(1) + conv2(0)
-    block = total.astype(BF16).astype(F32).reshape(FR, 6, COLS, CMID)
-    for f in range(FR):
-        a = jnp.concatenate(
-            [block[f, 0:1] * keep_top, block[f, 1:5], block[f, 5:6] * keep_bottom], axis=0
-        )
-        x3[f] = jnp.concatenate(shifted(a), axis=-1).astype(BF16)
-
-    for a in range(2):
-        window = jnp.concatenate(
-            [x3[:, a : a + ROWS], x3[:, a + 1 : a + 1 + ROWS]], axis=-1
-        ).reshape(FR * ROWS * COLS, 6 * CMID)
-        res = jnp.dot(window, wres[a], preferred_element_type=F32)
-        res = res.astype(BF16).reshape(FR, ROWS, COLS, 2 * COUT)
-        out_v[:, :, a] = res
-    store = pltpu.make_async_copy(out_v, out, load_sem.at[5])
-    store.start()
+    stores.append(finish(0, conv2(0, (0, 1), acc2[:two])))
 
     pair.wait_send()
     for copy in halos + halos2:
@@ -535,7 +556,8 @@
 
     for k in range(blocks):
         halves(k, functools.partial(drain, k))
-    store.wait()
+    for store in stores:
+        store.wait()
 
 
 def span_start(clips, tm):
@@ -567,15 +589,15 @@
             pltpu.VMEM((27, SHARD, CMID), BF16),
             pltpu.VMEM((UNITS, NZ, UNIT, 128), BF16),
             pltpu.VMEM((NY, YU, NZ, UNIT, 128), BF16),
-            pltpu.VMEM((27, CMID, CMID), BF16),
+            pltpu.VMEM((27, PAD, CMID), BF16),
             pltpu.VMEM((CMID, CIN), BF16),
             pltpu.VMEM((3, 3, CMID, COUT), BF16),
             pltpu.VMEM((6, 6, COLS, 3 * CIN), BF16),
             pltpu.VMEM((FR, ROWS, COLS, CMID), F32),
             pltpu.VMEM((6, 8, COLS, CMID), BF16),
-            pltpu.VMEM((6, 8, COLS, 3 * CMID), BF16),
-            pltpu.VMEM((FR, 6, COLS, 3 * CMID), BF16),
-            pltpu.VMEM((2, 6 * CMID, 2 * COUT), BF16),
+            pltpu.VMEM((6, 8, COLS, 3 * PAD), BF16),
+            pltpu.VMEM((FR, 6, COLS, 3 * PAD), BF16),
+            pltpu.VMEM((2, 2, 3 * PAD, 2 * COUT), BF16),
             pltpu.VMEM((2, FR * ROWS * COLS, 256), F32),
             pltpu.VMEM((FR, ROWS, 2, COLS, 2 * COUT), BF16),
             pltpu.VMEM((FR * 6 * COLS, CMID), F32),
@@ -591,7 +613,7 @@
             pltpu.VMEM((128, CIN), BF16),
             pltpu.VMEM((CMID, 128), BF16),
             pltpu.VMEM((128, CMID), BF16),
-            dma((6,)),
+            dma((7,)),
             dma((2, 5)), dma((2, 5)),
             dma((2, 2)), dma((2, 2)),
             dma((1,)), dma((1,)),

time: 52.8 us -> 51.1 us (0.968)
  Pallas kernels: 51 us -> 49.3 us
    pallas_call x1, Pallas kernels: 51 us -> 49.3 us  [shards(): pl.pallas_call(kernel, out_shape=jax.ShapeDtypeStruct((FR, ROWS, 2, COLS,...]
where the time goes in v5:
time: 51.1 us; the launch traced here: 50.9 us
  Pallas kernels  49.3 us (96%)
  local copies, waits for them, and re-layouts  1.67 us (3%)
    pallas_call x1, Pallas kernels, shards(): pl.pallas_call(kernel, out_shape=jax.ShapeDtypeStruct((FR, ROWS, 2, COLS,...  49.3 us
    unnamed x1, local copies, waits for them, and re-layouts  1.67 us

profile of v5, /device:TPU:1, one launch (start us, length us, event | category | flops | bytes accessed | tf_op | source)
XLA Modules:
  0.0 50.9 jit_solution(14286497183674846320)
XLA Ops:
  0.0 49.3 %shard_map.100 = bf16[4,4,2,16,192]{4,3,2,1,0:T(8,128)(2,1)} custom-call(bf16[4,4,16,384]{3,2,1,0:T(8,128)(2,1)} %lat.1, f32[384]{0:T(512)} %g1.1, f32[384]{0:T(512)} %b1.1, bf16[27,24,192]{2,1,0:T(8,128)(2,1)} %bitcast.10, f32[192]{0:T(256)} %g2.1, f32[192]{0:T(256)} %b2.1, bf16[27,192,192]{2,1,0:T(8,128)(2,1)} %bitcast.8, bf16[192,384]{1,0:T(8,128)(2,1)} %bitcast.11, ...), custom_call_target="tpu_custom_call" | custom-call | tf_op jit(solution)/shard_map/pallas_call | solution.py:581
  49.3 1.7 %copy.12 = bf16[4,8,16,192]{3,2,1,0:T(8,128)(2,1)} copy(bf16[4,8,16,192]{3,2,1,0:T(8,128)(2,1)} %bitcast.9) | data formatting | bytes 393216

commit v6 on v5

--- a/solution.py
+++ b/solution.py
@@ -83,8 +83,8 @@
 
 
 def kernel(
-    lat, g1, b1, fk, g2, b2, sk, skw, rk, clips, out,
-    xraw, fk_in, fk_pair, w1, wy, w2, wskip, rkv, x1, hown, hraw, x2, x3, wres, acc_ref, out_v, acc2,
+    lat, g1_in, b1_in, fk, g2_in, b2_in, sk, skw, rk, clips_in, out,
+    clips, g1, b1, g2, b2, xraw, fk_in, fk_pair, w1, wy, w2, wskip, rkv, x1, hown, hraw, x2, x3, wres, acc_ref, acc2,
     mine, st_in, st_total, st_prev, mine2, st_in2, st_total2, st_prev2,
     lanes1, chans1, lanes2, chans2,
     load_sem, halo_s, halo_r, stat_s, stat_r, pair_s, pair_r,
@@ -120,6 +120,11 @@
         pltpu.make_async_copy(sk, w2.at[:, :CMID], load_sem.at[2]),
         pltpu.make_async_copy(skw, wskip, load_sem.at[3]),
         pltpu.make_async_copy(rk, rkv, load_sem.at[4]),
+        pltpu.make_async_copy(g1_in, g1, load_sem.at[5]),
+        pltpu.make_async_copy(b1_in, b1, load_sem.at[6]),
+        pltpu.make_async_copy(g2_in, g2, load_sem.at[7]),
+        pltpu.make_async_copy(b2_in, b2, load_sem.at[8]),
+        pltpu.make_async_copy(clips_in, clips, load_sem.at[9]),
     ]
     for load in loads:
         load.start()
@@ -177,7 +182,8 @@
                 wres[a, tap, d * PAD : d * PAD + CMID] = cols[d].astype(BF16)
                 wres[a, tap, d * PAD + CMID : (d + 1) * PAD] = jnp.zeros((PAD - CMID, 2 * COUT), BF16)
 
-    loads[1].wait()
+    for load in (loads[1], *loads[5:]):
+        load.wait()
     pl.semaphore_wait(barrier, TILES - 1 + len(near))
 
     def exchange(src, at_in, phase):
@@ -516,19 +522,14 @@
                 window = x3[frames : frames + 2, a + tap : a + tap + ROWS].reshape(2 * ROWS * COLS, 3 * PAD)
                 term = jnp.dot(window, wres[a, tap], preferred_element_type=F32)
                 res = term if res is None else res + term
-            out_v[frames : frames + 2, :, a] = res.astype(BF16).reshape(2, ROWS, COLS, 2 * COUT)
-        store = pltpu.make_async_copy(
-            out_v.at[frames : frames + 2], out.at[frames : frames + 2], load_sem.at[5 + frames // 2]
-        )
-        store.start()
-        return store
+            out[frames : frames + 2, :, a] = res.astype(BF16).reshape(2, ROWS, COLS, 2 * COUT)
 
     two = 2 * 6 * COLS
     gain, bias = g2[...].reshape(1, CMID), b2[...].reshape(1, CMID)
     scale, shift = affine(st_total2[...], gain, bias, CMID // GROUPS, chans2[...])
     for f in range(FR):
         second_act(2 + f, scale[f], shift[f])
-    stores = [finish(2, conv2(2, (0, 1, 2), acc2[two:]))]
+    finish(2, conv2(2, (0, 1, 2), acc2[two:]))
     acc2[:two] = conv2(0, (2,), acc2[:two])
     relayed2.wait_recv()
     for copy in halos2[2:]:
@@ -536,7 +537,7 @@
     scale, shift = affine(st_prev2[...], gain, bias, CMID // GROUPS, chans2[...])
     second_act(0, scale[2], shift[2])
     second_act(1, scale[3], shift[3])
-    stores.append(finish(0, conv2(0, (0, 1), acc2[:two])))
+    finish(0, conv2(0, (0, 1), acc2[:two]))
 
     pair.wait_send()
     for copy in halos + halos2:
@@ -556,8 +557,6 @@
 
     for k in range(blocks):
         halves(k, functools.partial(drain, k))
-    for store in stores:
-        store.wait()
 
 
 def span_start(clips, tm):
@@ -574,16 +573,21 @@
 ):
     fk = jnp.transpose(first_kernel, (1, 2, 3, 0, 4)).reshape(27, SHARD, CMID)
     sk = jnp.transpose(second_kernel, (1, 2, 3, 0, 4)).reshape(27, CMID, CMID)
-    anywhere = pl.BlockSpec(memory_space=pl.ANY)
+    in_hbm = pl.BlockSpec(memory_space=pltpu.HBM)
     vmem = pl.BlockSpec(memory_space=pltpu.VMEM)
-    smem = pl.BlockSpec(memory_space=pltpu.SMEM)
     dma = pltpu.SemaphoreType.DMA
+    operands = (
+        latents, first_gain, first_bias, fk, second_gain, second_bias, sk, skip_weight.T, resample_kernel, clip_spans,
+    )
     out = pl.pallas_call(
         kernel,
         out_shape=jax.ShapeDtypeStruct((FR, ROWS, 2, COLS, 2 * COUT), BF16),
-        in_specs=[anywhere, vmem, vmem, anywhere, vmem, vmem, anywhere, anywhere, anywhere, smem],
-        out_specs=anywhere,
+        in_specs=[in_hbm] * len(operands),
+        out_specs=vmem,
         scratch_shapes=[
+            pltpu.SMEM((4,), jnp.int32),
+            pltpu.VMEM((CIN,), F32), pltpu.VMEM((CIN,), F32),
+            pltpu.VMEM((CMID,), F32), pltpu.VMEM((CMID,), F32),
             pltpu.VMEM((6, 6, COLS, CIN), BF16),
             pltpu.VMEM((27, SHARD, CMID), BF16),
             pltpu.VMEM((27, SHARD, CMID), BF16),
@@ -599,7 +603,6 @@
             pltpu.VMEM((FR, 6, COLS, 3 * PAD), BF16),
             pltpu.VMEM((2, 2, 3 * PAD, 2 * COUT), BF16),
             pltpu.VMEM((2, FR * ROWS * COLS, 256), F32),
-            pltpu.VMEM((FR, ROWS, 2, COLS, 2 * COUT), BF16),
             pltpu.VMEM((FR * 6 * COLS, CMID), F32),
             pltpu.VMEM((2, 128), F32),
             pltpu.VMEM((TILES - 1, 2, 128), F32),
@@ -613,7 +616,7 @@
             pltpu.VMEM((128, CIN), BF16),
             pltpu.VMEM((CMID, 128), BF16),
             pltpu.VMEM((128, CMID), BF16),
-            dma((7,)),
+            dma((10,)),
             dma((2, 5)), dma((2, 5)),
             dma((2, 2)), dma((2, 2)),
             dma((1,)), dma((1,)),
@@ -623,13 +626,9 @@
             dma((4, 6)), dma((4, 6)),
         ],
         compiler_params=pltpu.CompilerParams(
-            collective_id=0, has_side_effects=True, vmem_limit_bytes=56 * 2**20
+            collective_id=0, has_side_effects=True, vmem_limit_bytes=28 * 2**20
         ),
-    )(
-        latents, first_gain, first_bias, fk,
-        second_gain, second_bias, sk, skip_weight.T,
-        resample_kernel, clip_spans,
-    )
+    )(*[pltpu.with_memory_space_constraint(operand, pltpu.HBM) for operand in operands])
     return out.reshape(FR, 2 * ROWS, COLS, 2 * COUT)
 
 

time: 51.1 us -> 48.9 us (0.957)
  Pallas kernels: 49.3 us -> 48 us
  local copies, waits for them, and re-layouts: 1.67 us -> 0.71 us
    pallas_call x1, Pallas kernels: 49.3 us -> 48 us  [shards(): pl.pallas_call(kernel, out_shape=jax.ShapeDtypeStruct((FR, ROWS, 2, COLS,...]
    unnamed x1, local copies, waits for them, and re-layouts: 1.67 us -> 0.71 us
where the time goes in v6:
time: 48.9 us; the launch traced here: 48.7 us
  Pallas kernels  48 us (98%)
  local copies, waits for them, and re-layouts  0.71 us (1%)
    pallas_call x1, Pallas kernels, shards(): pl.pallas_call(kernel, out_shape=jax.ShapeDtypeStruct((FR, ROWS, 2, COLS,...  48 us

profile of v6, /device:TPU:1, one launch (start us, length us, event | category | flops | bytes accessed | tf_op | source)
XLA Modules:
  0.0 48.7 jit_solution(10196850391142950813)
XLA Ops:
  0.0 48.0 %shard_map.100 = bf16[4,4,2,16,192]{4,3,2,1,0:T(8,128)(2,1)S(1)} custom-call(bf16[4,4,16,384]{3,2,1,0:T(8,128)(2,1)} %lat.1, f32[384]{0:T(512)} %g1_in.1, f32[384]{0:T(512)} %b1_in.1, bf16[27,24,192]{2,1,0:T(8,128)(2,1)} %bitcast.10, f32[192]{0:T(256)} %g2_in.1, f32[192]{0:T(256)} %b2_in.1, bf16[27,192,192]{2,1,0:T(8,128)(2,1)} %bitcast.9, ...), custom_call_target="tpu_custom_call" | custom-call | tf_op jit(solution)/shard_map/pallas_call | solution.py:582
  48.0 0.7 %copy.12 = bf16[4,8,16,192]{3,2,1,0:T(8,128)(2,1)} copy(bf16[4,8,16,192]{3,2,1,0:T(8,128)(2,1)S(1)} %bitcast.8) | data formatting | bytes 393216

commit v7 on v6

--- a/solution.py
+++ b/solution.py
@@ -24,6 +24,9 @@
 ZT = UNITS - XT - YT
 PAD = 256
 HEIGHT = ROWS * TILES
+
+
+FAR_FIRST = sorted(range(1, TILES), key=lambda i: -min(i, TILES - i))
 
 
 def member(per, transposed):
@@ -114,6 +117,18 @@
             device_id=to, device_id_type=pl.DeviceIdType.MESH,
         )
 
+    barrier = pltpu.get_barrier_semaphore()
+    near = [along_x(1), along_x(-1), along_y(1), along_y(-1), along_y(2), along_y(-2)]
+    near += [(tm_prev, tile), (tm_prev, up), (tm_prev, down)]
+
+    def greet(to):
+        pl.semaphore_signal(barrier, inc=1, device_id=to, device_id_type=pl.DeviceIdType.MESH)
+
+    for i in FAR_FIRST:
+        greet((tm, lax.rem(tile + i, TILES)))
+    for to in near:
+        greet(to)
+
     loads = [
         pltpu.make_async_copy(lat, xraw.at[2:6, 1:5], load_sem.at[0]),
         pltpu.make_async_copy(fk, fk_in, load_sem.at[1]),
@@ -128,21 +143,6 @@
     ]
     for load in loads:
         load.start()
-
-    barrier = pltpu.get_barrier_semaphore()
-    near = [along_x(1), along_x(-1), along_y(1), along_y(-1), along_y(2), along_y(-2)]
-    near += [(tm_prev, tile), (tm_prev, up), (tm_prev, down)]
-
-    def greet(to):
-        pl.semaphore_signal(barrier, inc=1, device_id=to, device_id_type=pl.DeviceIdType.MESH)
-
-    def greet_group(i, carry):
-        greet((tm, lax.rem(tile + i, TILES)))
-        return carry
-
-    lax.fori_loop(1, TILES, greet_group, 0)
-    for to in near:
-        greet(to)
 
     w2[:, CMID:] = jnp.zeros((27, PAD - CMID, CMID), BF16)
     for d in range(3):
@@ -187,12 +187,11 @@
     pl.semaphore_wait(barrier, TILES - 1 + len(near))
 
     def exchange(src, at_in, phase):
-        for far in range(8, 0, -1):
-            for i in (far, TILES - far)[: 2 if far < 8 else 1]:
-                remote(
-                    src, at_in.at[i - 1], stat_s.at[phase, 0], stat_r.at[phase, 0],
-                    (tm, lax.rem(tile + i, TILES)),
-                ).start()
+        for i in FAR_FIRST:
+            remote(
+                src, at_in.at[i - 1], stat_s.at[phase, 0], stat_r.at[phase, 0],
+                (tm, lax.rem(tile + i, TILES)),
+            ).start()
 
     def exchange_copy(at_in, phase):
         return remote(at_in, at_in, stat_s.at[phase, 0], stat_r.at[phase, 0], partner)

time: 48.9 us -> 49 us (level)
  no operation moved by 1% of the time
where the time goes in v7:
time: 49 us; the launch traced here: 48.9 us
  Pallas kernels  48.2 us (98%)
  local copies, waits for them, and re-layouts  0.71 us (1%)
    pallas_call x1, Pallas kernels, shards(): pl.pallas_call(kernel, out_shape=jax.ShapeDtypeStruct((FR, ROWS, 2, COLS,...  48.2 us

profile of v7, /device:TPU:1, one launch (start us, length us, event | category | flops | bytes accessed | tf_op | source)
XLA Modules:
  0.0 48.9 jit_solution(7016822958577030458)
XLA Ops:
  0.0 48.2 %shard_map.100 = bf16[4,4,2,16,192]{4,3,2,1,0:T(8,128)(2,1)S(1)} custom-call(bf16[4,4,16,384]{3,2,1,0:T(8,128)(2,1)} %lat.1, f32[384]{0:T(512)} %g1_in.1, f32[384]{0:T(512)} %b1_in.1, bf16[27,24,192]{2,1,0:T(8,128)(2,1)} %bitcast.10, f32[192]{0:T(256)} %g2_in.1, f32[192]{0:T(256)} %b2_in.1, bf16[27,192,192]{2,1,0:T(8,128)(2,1)} %bitcast.9, ...), custom_call_target="tpu_custom_call" | custom-call | tf_op jit(solution)/shard_map/pallas_call | solution.py:581
  48.2 0.7 %copy.12 = bf16[4,8,16,192]{3,2,1,0:T(8,128)(2,1)} copy(bf16[4,8,16,192]{3,2,1,0:T(8,128)(2,1)S(1)} %bitcast.8) | data formatting | bytes 393216
